TPU v7x, 32 devices: a whole 2x2x4 slice. The times are simulated.
32 devices in a mesh: dp: 16 (over z, y, core), code: 2 (over x).
Axes of the slice: x: 2, y: 2, z: 4, core: 2. Of those that a mesh axis runs over, the one named last changes fastest.
Arguments:
- encoded: bfloat16 [4096, 256], P('dp'), may hold values from -32 to 32
- codebook: bfloat16 [131072, 256], P('code'), may hold values from -2 to 2
Outputs:
- grad_rows: float32 [4096, 256], P('dp')
- grad_codes: float32 [131072, 256], P(('code', 'dp'))
All inputs are finite; a program needn't handle non-finite values.
Results may differ from a plain program's by a relative error of at most 0.0045.
Values may be sent and summed in bfloat16 or wider, within the bound.
No kernel may reach another device: no remote copies, remote signals or barrier semaphores. Data moves between devices by JAX's collectives and lax.ppermute only.
A program may use at most 128 MiB of HBM per device.

v0:
```python
import math

import jax
import jax.numpy as jnp
from jax import lax
from jax.sharding import PartitionSpec as P


def logit_block(encoded, code_rows, code_squares):
    scores = lax.dot_general(
        encoded, code_rows, (((1,), (1,)), ((), ())), preferred_element_type=jnp.float32
    )
    return scores - 0.5 * code_squares[None, :]


def grad_block(encoded, row_lse, entropy, cross_term, code_rows, code_squares, log_mass):
    logits = logit_block(encoded, code_rows, code_squares)
    weights = jnp.exp(logits - row_lse[:, None])
    shaped = weights * (
        row_lse[:, None] - logits - entropy[:, None] + log_mass[None, :] - cross_term[:, None]
    )
    return shaped.astype(jnp.bfloat16)


def code_term(grad_tile, encoded, code_rows):
    pulled = lax.dot_general(
        grad_tile, encoded, (((0,), (0,)), ((), ())), preferred_element_type=jnp.float32
    )
    totals = jnp.sum(grad_tile.astype(jnp.float32), axis=0)
    return pulled - totals[:, None] * code_rows.astype(jnp.float32)


def body(encoded, codebook):
    rows_here, features = encoded.shape
    codes_here = codebook.shape[0]
    block_size = math.gcd(codes_here, 2048)
    block_count = codes_here // block_size
    squares = jnp.sum(jnp.square(codebook.astype(jnp.float32)), axis=1)
    code_blocks = codebook.reshape(block_count, block_size, features)
    square_blocks = squares.reshape(block_count, block_size)
    row_zeros = jnp.zeros((rows_here,), jnp.float32)

    def online_step(running, inputs):
        run_max, run_sum, run_dot = running
        logits = logit_block(encoded, inputs[0], inputs[1])
        new_max = jnp.maximum(run_max, jnp.max(logits, axis=1))
        exponent = jnp.exp(logits - new_max[:, None])
        factor = jnp.exp(run_max - new_max)
        return (
            (
                new_max,
                run_sum * factor + jnp.sum(exponent, axis=1),
                run_dot * factor + jnp.sum(exponent * logits, axis=1),
            ),
            None,
        )

    start_state = (jnp.full((rows_here,), -jnp.inf, jnp.float32), row_zeros, row_zeros)
    (local_max, local_sum, local_dot), unused = lax.scan(
        online_step, start_state, (code_blocks, square_blocks)
    )
    row_max = lax.pmax(local_max, "code")
    factor = jnp.exp(local_max - row_max)
    row_sum, row_dot = lax.psum((local_sum * factor, local_dot * factor), "code")
    row_lse = row_max + jnp.log(row_sum)
    entropy = row_lse - row_dot / row_sum

    def mass_block(inputs):
        logits = logit_block(encoded, inputs[0], inputs[1])
        return jnp.sum(jnp.exp(logits - row_lse[:, None]), axis=0)

    local_mass = lax.map(mass_block, (code_blocks, square_blocks)).reshape(codes_here)
    total_rows = rows_here * lax.axis_size("dp")
    mean_mass = lax.psum(local_mass, "dp") / total_rows
    log_mass = jnp.log(mean_mass)
    log_blocks = log_mass.reshape(block_count, block_size)

    def cross_step(running, inputs):
        logits = logit_block(encoded, inputs[0], inputs[1])
        weights = jnp.exp(logits - row_lse[:, None])
        return (running + jnp.sum(weights * inputs[2][None, :], axis=1), None)

    local_cross, unused = lax.scan(cross_step, row_zeros, (code_blocks, square_blocks, log_blocks))
    cross_term = lax.psum(local_cross, "code")
    grad_start = jnp.zeros((rows_here, features), jnp.float32)

    def row_step(running, inputs):
        grad_tile = grad_block(
            encoded, row_lse, entropy, cross_term, inputs[0], inputs[1], inputs[2]
        )
        return (running + jnp.dot(grad_tile, inputs[0], preferred_element_type=jnp.float32), None)

    local_rows, unused = lax.scan(row_step, grad_start, (code_blocks, square_blocks, log_blocks))
    share = codes_here // lax.axis_size("dp")
    offset = lax.axis_index("dp") * share
    own_rows = lax.dynamic_slice_in_dim(codebook, offset, share, 0)
    own_squares = lax.dynamic_slice_in_dim(squares, offset, share, 0)
    own_logs = lax.dynamic_slice_in_dim(log_mass, offset, share, 0)
    all_lse, all_entropy, all_cross = (
        lax.all_gather(row_lse, "dp", axis=0, tiled=True),
        lax.all_gather(entropy, "dp", axis=0, tiled=True),
        lax.all_gather(cross_term, "dp", axis=0, tiled=True),
    )
    batch_rows = lax.all_gather(encoded, "dp", axis=0, tiled=True)
    grad_tile = grad_block(
        batch_rows, all_lse, all_entropy, all_cross, own_rows, own_squares, own_logs
    )
    grad_codes = code_term(grad_tile, batch_rows, own_rows)
    grad_rows = lax.psum(local_rows, "code")
    return (grad_rows, grad_codes)


def solution(mesh):
    placed = (P("dp", None), P("code", None))
    return jax.shard_map(
        body,
        mesh=mesh,
        in_specs=placed,
        out_specs=(P("dp", None), P(("code", "dp"), None)),
        check_vma=False,
    )
```

profile of v0, /device:TPU:0, one launch (start us, length us, event | category | flops | bytes accessed | tf_op | source)
XLA Modules:
  0.0 528.8 jit_solution(9168958207868606298)
XLA Ops:
  7.3 11.8 %multiply_reduce_fusion = f32[65536]{0:T(1024)S(1)} fusion(bf16[65536,256]{1,0:T(8,128)(2,1)} %param.11), kind=kLoop, calls=%fused_computation.52 | loop fusion | flops 50266112 | bytes 33816576 | tf_op jit(solution)/shard_map/reduce_sum | solution.py:38
  19.2 74.7 %while.48 = (s32[]{:T(128)}, f32[256]{0:T(256)S(1)}, f32[256]{0:T(256)S(1)}, f32[256]{0:T(256)S(1)}, bf16[32,2048,256]{2,1,0:T(8,128)(2,1)}, /*index=5*/bf16[256...) while((s32[]{:T(128)}, f32[256]{0:T(256)S(1)}, f32[256]{0:T(256)S(1)}, ...), condition=%wide.region_5.6_spmd.clone, body=%wide.region_1.5_spmd.clone.sunk | while | flops 271585024 | bytes 5416056 | solution.py:59
  93.9 5.8 %pmax.7 = f32[256]{0:T(256)S(1)} all-reduce(f32[256]{0:T(256)S(1)} %get-tuple-element.157), channel_id=1, replica_groups=mesh['dp'=16,'code'=2] {'code'}, use_global_device_ids=true, to_apply=%region_6.7 | all-reduce | flops 256 | bytes 2048 | tf_op jit(solution)/shard_map/pmax | solution.py:62
  99.8 4.9 psum.35
  104.7 65.8 %while.47 = (s32[]{:T(128)}, f32[32,2048]{1,0:T(8,128)S(1)}, bf16[32,2048,256]{2,1,0:T(8,128)(2,1)}, bf16[256,256]{1,0:T(8,128)(2,1)S(1)}, f32[32,2048]{1,0:T(8,...) while((s32[]{:T(128)}, f32[32,2048]{1,0:T(8,128)S(1)}, bf16[32,2048,256]{2,1,0:T(8,128)(2,1)}, ...), condition=%wide.region_10.11_spmd, body=%wide.region_8.10_spmd.sunk | while | flops 270008320 | bytes 1229929 | solution.py:72
  172.1 22.2 %all-gather = f32[16,1,256]{2,1,0:T(1,128)S(1)} all-gather(f32[1,1,256]{2,1,0:T(1,128)S(1)} %bitcast.101), channel_id=1, replica_groups=mesh['dp'=16,'code'=2] {'dp'}, dimensions={0}, use_global_device_ids=true | all-gather | bytes 17408 | tf_op jit(solution)/shard_map/all_gather | solution.py:100
  194.3 67.6 %all-reduce.4.cloned.1.call-done = f32[65536]{0:T(1024)} async-done(((f32[65536]{0:T(1024)}), f32[65536]{0:T(1024)}) %all-reduce.4.cloned.1.call-update) | async-done | bytes 262160 | tf_op jit(solution)/shard_map/psum | solution.py:74
  263.0 63.1 %while.49 = (s32[]{:T(128)}, f32[256]{0:T(256)S(1)}, bf16[32,2048,256]{2,1,0:T(8,128)(2,1)}, bf16[256,256]{1,0:T(8,128)(2,1)}, f32[32,2048]{1,0:T(8,128)S(1)}, /...) while((s32[]{:T(128)}, f32[256]{0:T(256)S(1)}, ...), condition=%wide.region_15.16_spmd.clone, body=%wide.region_13.15_spmd.clone.sunk | while | flops 270534912 | bytes 1234039 | solution.py:83
  326.2 4.9 all-reduce
  331.1 103.3 %while.50 = (s32[]{:T(128)}, f32[256,256]{1,0:T(8,128)S(1)}, bf16[32,2048,256]{2,1,0:T(8,128)(2,1)}, bf16[256,256]{1,0:T(8,128)(2,1)}, f32[32,2048]{1,0:T(8,128)...) while((s32[]{:T(128)}, f32[256,256]{1,0:T(8,128)S(1)}, ...), condition=%wide.region_18.19_spmd.clone, body=%wide.region_17.18_spmd.clone.sunk | while | flops 541198336 | bytes 2806402 | solution.py:93
  331.1 3.2 convolution_add_fusion.2
  337.6 3.2 convolution_add_fusion.2
  340.8 3.2 convolution_add_fusion.2
  350.5 3.2 convolution_add_fusion.2
  357.0 3.2 convolution_add_fusion.2
  360.2 3.1 convolution_add_fusion.2
  363.4 3.2 convolution_add_fusion.2
  366.6 3.3 convolution_add_fusion.2
  376.3 3.2 convolution_add_fusion.2
  379.6 3.2 convolution_add_fusion.2
  386.1 3.2 convolution_add_fusion.2
  389.3 3.2 convolution_add_fusion.2
  395.8 3.1 convolution_add_fusion.2
  402.2 3.2 convolution_add_fusion.2
  408.6 3.2 convolution_add_fusion.2
  415.0 3.2 convolution_add_fusion.2
  418.3 3.2 convolution_add_fusion.2
  421.6 3.2 convolution_add_fusion.2
  434.4 20.9 %all-gather.2 = f32[16,1,256]{2,1,0:T(1,128)S(1)} all-gather(f32[1,1,256]{2,1,0:T(1,128)S(1)} %bitcast.103), channel_id=1, replica_groups=mesh['dp'=16,'code'=2] {'dp'}, dimensions={0}, use_global_device_ids=true | all-gather | bytes 17408 | tf_op jit(solution)/shard_map/all_gather | solution.py:102
  455.4 17.6 %all-gather.1 = f32[16,1,256]{2,1,0:T(1,128)S(1)} all-gather(f32[1,1,256]{2,1,0:T(1,128)S(1)} %bitcast.102), channel_id=1, replica_groups=mesh['dp'=16,'code'=2] {'dp'}, dimensions={0}, use_global_device_ids=true | all-gather | bytes 17408 | tf_op jit(solution)/shard_map/all_gather | solution.py:101
  473.0 29.8 %convert_reduce_fusion = (f32[4096]{0:T(1024)S(1)}, bf16[4096,4096]{0,1:T(8,128)(2,1)}) fusion(f32[4096]{0:T(1024)S(1)} %bitcast.99, f32[4096]{0:T(1024)S(1)} %dynamic_slice.43, f32[4096]{0:T(1024)S(1)} %bitcast.100, f32[4096]{0:T(1024)S(1)} %bitcast.98, f32[4096]{0:T(1024)S(1)} %dynamic-slice_multiply_fusion.4, ...), kind=kOutput, calls=%fused_computation.50 | convolution fusion | flops 8757702656 | bytes 37847044 | tf_op jit(solution)/shard_map/dot_general | solution.py:10
  502.8 17.8 %convolution_subtract_fusion.4 = f32[4096,256]{1,0:T(8,128)} fusion(bf16[4096,4096]{0,1:T(8,128)(2,1)} %get-tuple-element.314, bf16[4096,256]{1,0:T(8,128)(2,1)S(1)} %copy-done.3, f32[4096]{0:T(1024)S(1)} %get-tuple-element.313, bf16[65536,256]{1,0:T(8,128)(2,1)} %bitcast.88, s32[]{:T(128)S(6)} %select_n.2), kind=kOutput, calls=%fused_computation.53 | convolution fusion | flops 8593080320 | bytes 41959428 | tf_op jit(solution)/shard_map/dot_general | solution.py:26
  (462 shorter events, 249.3 us)
Async XLA Ops:
  7.2 254.8 %all-reduce.4.cloned.1.call-start = ((), (), s32[]{:S(2)}) async-start(), calls=%async_computation | async-start | bytes 524288 | tf_op jit(solution)/shard_map/psum | solution.py:74
  7.2 11.9 %copy-start = (bf16[256,256]{1,0:T(8,128)(2,1)S(1)}, bf16[256,256]{1,0:T(8,128)(2,1)}, u32[]{:S(2)}) copy-start(bf16[256,256]{1,0:T(8,128)(2,1)} %param.10) | copy-start | bytes 393220
  170.5 0.8 copy-start.1
  171.3 301.7 %all-gather.5.cloned.1.call-start = ((), (), s32[]{:S(2)}) async-start(), calls=%async_computation.2 | async-start | bytes 2228224 | tf_op jit(solution)/shard_map/all_gather | solution.py:104
  172.0 348.6 %all-reduce.6.cloned.1.call-start = ((), (), s32[]{:S(2)}) async-start(), calls=%async_computation.1 | async-start | bytes 524288 | tf_op jit(solution)/shard_map/psum | solution.py:109
  434.4 38.6 %copy-start.2 = (f32[256,256]{1,0:T(8,128)}, f32[256,256]{1,0:T(8,128)S(1)}, u32[]{:S(2)}) copy-start(f32[256,256]{1,0:T(8,128)S(1)} %get-tuple-element.162) | copy-start | bytes 786436
  473.0 29.8 %copy-start.3 = (bf16[4096,256]{1,0:T(8,128)(2,1)S(1)}, bf16[4096,256]{1,0:T(8,128)(2,1)}, u32[]{:S(2)}) copy-start(bf16[4096,256]{1,0:T(8,128)(2,1)} %all-gather.5.cloned.1.call-done) | copy-start | bytes 6291460
Sparse Core Ops, SparseCore 0:
  171.4 90.5 all-reduce.3
  264.7 41.8 all-gather.4
  473.1 21.5 all-reduce.5
where the time goes:
time: 533 us; the launch traced here: 529 us
  matrix products  325 us (61%)
  blocking collectives  76.5 us (14%)
  waiting for transfers between devices  68.4 us (13%)
  other arithmetic  31.7 us (6%)
  between operations  13.9 us (3%)
  local copies, waits for them, and re-layouts  9.16 us (2%)
    dot_general x97, matrix products, logit_block(): lax.dot_general(encoded, code_rows, (((1,), (1,)), ((), ())), preferred_e...  205 us
    dot_general x32, matrix products, row_step(): jnp.dot(grad_tile, inputs[0], preferred_element_type=jnp.float32)  101 us
    psum x1, waiting for transfers between devices, body(): mean_mass = lax.psum(local_mass, 'dp') / total_rows  67.6 us
    all_gather x1, blocking collectives, body(): lax.all_gather(row_lse, 'dp', axis=0, tiled=True)  22.2 us
    all_gather x1, blocking collectives, body(): lax.all_gather(cross_term, 'dp', axis=0, tiled=True)  20.9 us
    dot_general x1, matrix products, code_term(): lax.dot_general(grad_tile, encoded, (((0,), (0,)), ((), ())), preferred_e...  17.8 us
    all_gather x1, blocking collectives, body(): lax.all_gather(entropy, 'dp', axis=0, tiled=True)  17.6 us
    reduce_sum x32, other arithmetic, online_step(): jnp.sum(exponent * logits, axis=1)  15.1 us
  transfers between devices with their start and end apart: 3, of which 1 were waited for; matrix products, arithmetic and copies ran while one was open for 40% of the time, Pallas kernels for 0%

commit v1 on v0

v1 whole, which is shorter than its diff:
```python
import math

import jax
import jax.numpy as jnp
from jax import lax
from jax.experimental import pallas as pl
from jax.experimental.pallas import tpu as pltpu
from jax.sharding import PartitionSpec as P

LOG2E = math.log2(math.e)
LN2 = math.log(2.0)
LOG2LN2 = math.log2(LN2)
LANES = 128
PARAMS = pltpu.CompilerParams(vmem_limit_bytes=56 * 2**20)
NT = (((1,), (1,)), ((), ()))


def half_squares(code_rows):
    values = code_rows.astype(jnp.float32)
    return jnp.sum(values * values, axis=1, keepdims=True) * (0.5 * LOG2E)


def column_to_row(column):
    wide = jnp.broadcast_to(column, (column.shape[0], LANES))
    return jnp.transpose(wide)[0:1, :]


def stats_call(encoded_t, codebook):
    features, rows = encoded_t.shape
    codes = codebook.shape[0]
    block = math.gcd(codes, 8192)
    chunk = math.gcd(block, 256)

    def kernel(encoded_ref, codes_ref, max_ref, sum_ref, top, total):
        step = pl.program_id(0)

        @pl.when(step == 0)
        def _():
            top[...] = jnp.full(top.shape, -3e38, jnp.float32)
            total[...] = jnp.zeros(total.shape, jnp.float32)

        run_max, run_sum = top[...], total[...]
        for k in range(block // chunk):
            code_rows = codes_ref[k * chunk : (k + 1) * chunk, :]
            scores = jnp.dot(code_rows, encoded_ref[...], preferred_element_type=jnp.float32)
            logits = (scores * LOG2E - half_squares(code_rows)).reshape(chunk // 8, 8, rows)
            new_max = jnp.maximum(run_max, jnp.max(logits, axis=0))
            powers = jnp.exp2(logits - new_max[None])
            run_sum = run_sum * jnp.exp2(run_max - new_max) + jnp.sum(powers, axis=0)
            run_max = new_max
        top[...] = run_max
        total[...] = run_sum

        @pl.when(step == pl.num_programs(0) - 1)
        def _():
            row_max = jnp.max(run_max, axis=0, keepdims=True)
            max_ref[...] = row_max
            sum_ref[...] = jnp.sum(run_sum * jnp.exp2(run_max - row_max), axis=0, keepdims=True)

    out = jax.ShapeDtypeStruct((1, rows), jnp.float32)
    return pl.pallas_call(
        kernel,
        grid=(codes // block,),
        in_specs=[
            pl.BlockSpec((features, rows), lambda i: (0, 0)),
            pl.BlockSpec((block, features), lambda i: (i, 0)),
        ],
        out_specs=[pl.BlockSpec((1, rows), lambda i: (0, 0))] * 2,
        out_shape=[out, out],
        scratch_shapes=[pltpu.VMEM((8, rows), jnp.float32)] * 2,
        compiler_params=PARAMS,
        name="row_stats",
    )(encoded_t, codebook)


def place_of(offset, count):
    bits = count.bit_length() - 1
    return sum(((offset >> b) & 1) << (bits - 1 - b) for b in range(bits))


def mass_call(me, batch_rows, codebook, all_lse, devices, own):
    total_rows, features = batch_rows.shape
    rows = total_rows // devices
    block = math.gcd(own, 256)
    blocks = own // block

    def kernel(me_ref, rows_ref, codes_ref, lse_ref, log_ref, cross_ref, logits_scr):
        step = pl.program_id(0)

        @pl.when(step == 0)
        def _():
            cross_ref[...] = jnp.zeros(cross_ref.shape, jnp.float32)

        code_rows = codes_ref[...]
        squares = half_squares(code_rows)
        mass = jnp.zeros((block, rows), jnp.float32)
        for d in range(devices):
            part = slice(d * rows, (d + 1) * rows)
            scores = lax.dot_general(code_rows, rows_ref[part, :], NT, preferred_element_type=jnp.float32)
            place = place_of(me_ref[0] ^ d, devices)
            logits = scores * LOG2E - squares - lse_ref[pl.ds(place, 1), :]
            weights = jnp.exp2(logits)
            mass = mass + weights
            logits_scr[:, part] = logits
        log_mass = jnp.log2(jnp.sum(mass, axis=1, keepdims=True) * (1.0 / (LN2 * total_rows)))
        log_ref[...] = column_to_row(log_mass)
        for d in range(devices):
            part = slice(d * rows, (d + 1) * rows)
            logits = logits_scr[:, part]
            terms = jnp.exp2(logits) * (log_mass - logits)
            cross_ref[:, part] += jnp.sum(terms.reshape(block // 8, 8, rows), axis=0)

    return pl.pallas_call(
        kernel,
        grid_spec=pltpu.PrefetchScalarGridSpec(
            num_scalar_prefetch=1,
            grid=(blocks,),
            in_specs=[
                pl.BlockSpec((total_rows, features), lambda i, me: (0, 0)),
                pl.BlockSpec((block, features), lambda i, me: (me[0] * blocks + i, 0)),
                pl.BlockSpec((devices, rows), lambda i, me: (0, 0)),
            ],
            out_specs=[
                pl.BlockSpec((1, block), lambda i, me: (0, i)),
                pl.BlockSpec((8, total_rows), lambda i, me: (0, 0)),
            ],
            scratch_shapes=[pltpu.VMEM((block, total_rows), jnp.float32)],
        ),
        out_shape=[
            jax.ShapeDtypeStruct((1, own), jnp.float32),
            jax.ShapeDtypeStruct((8, total_rows), jnp.float32),
        ],
        compiler_params=PARAMS,
        name="code_mass",
    )(me, batch_rows, codebook, all_lse)


def rows_call(me, encoded, codebook, lse_wide, shift_wide, all_squares, all_log, devices, own):
    rows, features = encoded.shape
    codes = codebook.shape[0]
    block = math.gcd(own, 4096)
    per_device = own // block
    chunk = math.gcd(block, 512)

    def kernel(me_ref, encoded_ref, codes_ref, lse_ref, shift_ref, squares_ref, log_ref, out_ref):
        @pl.when(pl.program_id(0) == 0)
        def _():
            out_ref[...] = jnp.zeros(out_ref.shape, jnp.float32)

        encoded_here = encoded_ref[...]
        total = out_ref[...]
        for k in range(block // chunk):
            part = slice(k * chunk, (k + 1) * chunk)
            code_rows = codes_ref[part, :]
            scores = lax.dot_general(encoded_here, code_rows, NT, preferred_element_type=jnp.float32)
            squares = squares_ref[0, :, part]
            log_mass = log_ref[0, :, part]
            tiles = []
            for q in range(chunk // LANES):
                lane = slice(q * LANES, (q + 1) * LANES)
                logits = scores[:, lane] * LOG2E - squares[:, lane] - lse_ref[...]
                tile = jnp.exp2(logits) * (log_mass[:, lane] - logits + shift_ref[...])
                tiles.append(tile.astype(jnp.bfloat16))
            grad_tile = jnp.concatenate(tiles, axis=1)
            total = total + jnp.dot(grad_tile, code_rows, preferred_element_type=jnp.float32)
        out_ref[...] = total

    def vector_map(i, me):
        return (place_of(me[0] ^ (i // per_device), devices), 0, i % per_device)

    return pl.pallas_call(
        kernel,
        grid_spec=pltpu.PrefetchScalarGridSpec(
            num_scalar_prefetch=1,
            grid=(codes // block,),
            in_specs=[
                pl.BlockSpec((rows, features), lambda i, me: (0, 0)),
                pl.BlockSpec((block, features), lambda i, me: (i, 0)),
                pl.BlockSpec((rows, LANES), lambda i, me: (0, 0)),
                pl.BlockSpec((rows, LANES), lambda i, me: (0, 0)),
                pl.BlockSpec((1, 1, block), vector_map),
                pl.BlockSpec((1, 1, block), vector_map),
            ],
            out_specs=pl.BlockSpec((rows, features), lambda i, me: (0, 0)),
        ),
        out_shape=jax.ShapeDtypeStruct((rows, features), jnp.float32),
        compiler_params=PARAMS,
        name="grad_rows",
    )(me, encoded, codebook, lse_wide, shift_wide, all_squares, all_log)


def codes_call(me, batch_rows, codebook, all_lse, shift, log_mass, devices, own):
    total_rows, features = batch_rows.shape
    rows = total_rows // devices
    block = math.gcd(own, 512)
    blocks = own // block

    def kernel(me_ref, rows_ref, codes_ref, lse_ref, shift_ref, log_ref, out_ref):
        log_mass = jnp.transpose(jnp.broadcast_to(log_ref[...], (LANES, block)))[:, 0:1]
        code_rows = codes_ref[...]
        squares = half_squares(code_rows)
        total = jnp.zeros((block, features), jnp.float32)
        sums = jnp.zeros((block, rows), jnp.float32)
        for d in range(devices):
            part = slice(d * rows, (d + 1) * rows)
            row_block = rows_ref[part, :]
            scores = lax.dot_general(code_rows, row_block, NT, preferred_element_type=jnp.float32)
            place = place_of(me_ref[0] ^ d, devices)
            logits = scores * LOG2E - squares - lse_ref[pl.ds(place, 1), :]
            tile = jnp.exp2(logits) * (log_mass - logits + shift_ref[:, part])
            sums = sums + tile
            total = total + jnp.dot(
                tile.astype(jnp.bfloat16), row_block, preferred_element_type=jnp.float32
            )
        code_sums = jnp.sum(sums, axis=1, keepdims=True)
        out_ref[...] = total - code_sums * code_rows.astype(jnp.float32)

    return pl.pallas_call(
        kernel,
        grid_spec=pltpu.PrefetchScalarGridSpec(
            num_scalar_prefetch=1,
            grid=(blocks,),
            in_specs=[
                pl.BlockSpec((total_rows, features), lambda i, me: (0, 0)),
                pl.BlockSpec((block, features), lambda i, me: (me[0] * blocks + i, 0)),
                pl.BlockSpec((devices, rows), lambda i, me: (0, 0)),
                pl.BlockSpec((1, total_rows), lambda i, me: (0, 0)),
                pl.BlockSpec((1, block), lambda i, me: (0, i)),
            ],
            out_specs=pl.BlockSpec((block, features), lambda i, me: (i, 0)),
        ),
        out_shape=jax.ShapeDtypeStruct((own, features), jnp.float32),
        compiler_params=PARAMS,
        name="grad_codes",
    )(me, batch_rows, codebook, all_lse, shift, log_mass)


def from_xor(values, axis, offset):
    return lax.ppermute(values, axis, [(i, i ^ offset) for i in range(lax.axis_size(axis))])


def xor_gather(values, axis):
    held = values[None]
    offset = lax.axis_size(axis) // 2
    while offset:
        held = jnp.concatenate([held, from_xor(held, axis, offset)], axis=0)
        offset //= 2
    return held


def xor_sum(values, axis):
    offset = lax.axis_size(axis) // 2
    while offset:
        values = values + from_xor(values, axis, offset)
        offset //= 2
    return values


def body(encoded, codebook):
    rows, features = encoded.shape
    codes = codebook.shape[0]
    devices = lax.axis_size("dp")
    own = codes // devices
    me_index = lax.axis_index("dp")
    me = me_index.astype(jnp.int32).reshape(1)

    batch_rows = lax.all_gather(encoded, "dp", axis=0, tiled=True)
    own_codes = lax.dynamic_slice_in_dim(codebook, me_index * own, own, 0).astype(jnp.float32)
    own_squares = jnp.sum(own_codes * own_codes, axis=1) * (0.5 * LOG2E)

    row_max, row_sum = stats_call(encoded.T, codebook)
    stats = jnp.concatenate([row_max, row_sum], axis=0)
    offset = lax.axis_size("code") // 2
    while offset:
        other = from_xor(stats, "code", offset)
        top = jnp.maximum(stats[0:1], other[0:1])
        total = stats[1:2] * jnp.exp2(stats[0:1] - top) + other[1:2] * jnp.exp2(other[0:1] - top)
        stats = jnp.concatenate([top, total], axis=0)
        offset //= 2
    row_lse = (stats[0] + jnp.log2(stats[1])) - LOG2LN2

    gathered = xor_gather(jnp.concatenate([row_lse, own_squares]), "dp")
    all_lse, all_squares = gathered[:, :rows], gathered[:, None, rows:]

    log_mass, cross = mass_call(me, batch_rows, codebook, all_lse, devices, own)
    cross = xor_sum(jnp.sum(cross, axis=0), "code")
    gathered = xor_gather(jnp.concatenate([log_mass[0], cross]), "dp")
    all_log = gathered[:, None, :own]
    shift = jnp.sum(gathered[:, own:], axis=0) * (-1.0 / LN2)
    own_shift = lax.dynamic_slice_in_dim(shift, me_index * rows, rows, 0)

    local_rows = rows_call(
        me,
        encoded,
        codebook,
        jnp.broadcast_to(row_lse[:, None], (rows, LANES)),
        jnp.broadcast_to(own_shift[:, None], (rows, LANES)),
        all_squares,
        all_log,
        devices,
        own,
    )
    grad_codes = codes_call(me, batch_rows, codebook, all_lse, shift[None, :], log_mass, devices, own)
    grad_rows = xor_sum(local_rows, "code")
    return grad_rows, grad_codes


def solution(mesh):
    placed = (P("dp", None), P("code", None))
    return jax.shard_map(
        body,
        mesh=mesh,
        in_specs=placed,
        out_specs=(P("dp", None), P(("code", "dp"), None)),
        check_vma=False,
    )
```

time: 533 us -> 181 us (0.34)
  matrix products: 325 us -> 0 us
  Pallas kernels: 0 us -> 115 us
  blocking collectives: 76.5 us -> 0 us
  waiting for transfers between devices: 68.4 us -> 20 us
  other arithmetic: 31.7 us -> 6.51 us
  starting transfers between devices: 0.12 us -> 18.4 us
    dot_general x130 -> x0, matrix products: 325 us -> none  [the longest x97 205 us: logit_block(): lax.dot_general(encoded, code_rows, (((1,), (1,)), ((), ())), preferred_e...]
    pallas_call x0 -> x4, Pallas kernels: none -> 115 us  [the longest x1 31 us: codes_call(): pl.pallas_call(kernel, grid_spec=pltpu.PrefetchScalarGridSpec(num_scalar_...]
    psum x2 -> x0, waiting for transfers between devices: 67.6 us -> none  [the longest x1 67.6 us: body(): mean_mass = lax.psum(local_mass, 'dp') / total_rows]
    all_gather x3 -> x0, blocking collectives: 60.7 us -> none  [the longest x1 22.2 us: body(): lax.all_gather(row_lse, 'dp', axis=0, tiled=True)]
    reduce_sum x33 -> x2, other arithmetic: 26.9 us -> 3.15 us  [the longest x1 2.21 us: body(): own_squares = jnp.sum(own_codes * own_codes, axis=1) * (0.5 * LOG2E)]
    ppermute x0 -> x11, waiting for transfers between devices: none -> 19.3 us  [from_xor(): lax.ppermute(values, axis, [(i, i ^ offset) for i in range(lax.axis_size(...]
    ppermute x0 -> x11, starting transfers between devices: none -> 18.3 us  [from_xor(): lax.ppermute(values, axis, [(i, i ^ offset) for i in range(lax.axis_size(...]
    psum x2 -> x0, blocking collectives: 9.88 us -> none  [body(): lax.psum((local_sum * factor, local_dot * factor), 'code')]
  transfers between devices with their start and end apart: 3 -> 12, of which waited for: 1 -> 9; matrix products, arithmetic and copies ran while one was open for 40% -> 4% of each run, Pallas kernels for 0% -> 32%
where the time goes in v1:
time: 181 us; the launch traced here: 180 us
  Pallas kernels  115 us (64%)
  waiting for transfers between devices  20 us (11%)
  starting transfers between devices  18.4 us (10%)
  between operations  14.1 us (8%)
  other arithmetic  6.51 us (4%)
  local copies, waits for them, and re-layouts  6.18 us (3%)
    pallas_call x1, Pallas kernels, codes_call(): pl.pallas_call(kernel, grid_spec=pltpu.PrefetchScalarGridSpec(num_scalar_...  31 us
    pallas_call x1, Pallas kernels, mass_call(): pl.pallas_call(kernel, grid_spec=pltpu.PrefetchScalarGridSpec(num_scalar_...  30.4 us
    pallas_call x1, Pallas kernels, stats_call(): pl.pallas_call(kernel, grid=(codes // block,), in_specs=[pl.BlockSpec((fe...  27 us
    pallas_call x1, Pallas kernels, rows_call(): pl.pallas_call(kernel, grid_spec=pltpu.PrefetchScalarGridSpec(num_scalar_...  26.7 us
    ppermute x11, waiting for transfers between devices, from_xor(): lax.ppermute(values, axis, [(i, i ^ offset) for i in range(lax.axis_size(...  19.3 us
    ppermute x11, starting transfers between devices, from_xor(): lax.ppermute(values, axis, [(i, i ^ offset) for i in range(lax.axis_size(...  18.3 us
  transfers between devices with their start and end apart: 12, of which 9 were waited for; matrix products, arithmetic and copies ran while one was open for 4% of the time, Pallas kernels for 32%

profile of v1, /device:TPU:0, one launch (start us, length us, event | category | flops | bytes accessed | tf_op | source)
XLA Modules:
  0.0 180.2 jit_solution(8975974004433110346)
XLA Ops:
  7.9 1.7 copy.4
  9.6 27.0 %row_stats.1 = (f32[1,256]{1,0:T(1,128)}, f32[1,256]{1,0:T(1,128)}) custom-call(bf16[256,256]{1,0:T(8,128)(2,1)} %bitcast.13, bf16[65536,256]{1,0:T(8,128)(2,1)} %codes_ref.7), custom_call_target="tpu_custom_call" | custom-call | tf_op jit(solution)/shard_map/row_stats/pallas_call | solution.py:61
  36.6 0.7 pad_maximum_fusion.8
  37.3 2.9 %collective-permute-start = (f32[2,256]{1,0:T(2,128)S(1)}, f32[2,256]{1,0:T(2,128)S(1)}, u32[]{:S(2)}, u32[]{:S(2)}) collective-permute-start(f32[2,256]{1,0:T(2,128)S(1)} %pad_maximum_fusion.8), channel_id=1, source_target_pairs={{0,1},{1,0},{2,3},{3,2},{4,5},{5,4},{6,7},{7,6},{8,9},{9,8},{10,11... | collective-permute-start | bytes 6152 | tf_op jit(solution)/shard_map/ppermute | solution.py:239
  40.2 2.2 %multiply_reduce_fusion = f32[4096]{0:T(1024)S(1)} fusion(bf16[65536,256]{1,0:T(8,128)(2,1)} %codes_ref.7, s32[]{:T(128)S(6)} %select_n.6), kind=kLoop, calls=%fused_computation | loop fusion | flops 3141632 | bytes 2113540 | tf_op jit(solution)/shard_map/reduce_sum | solution.py:269
  42.5 0.7 add_add_fusion
  43.2 2.6 %collective-permute-start.1 = (f32[1,4352]{1,0:T(1,128)S(1)}, f32[1,4352]{1,0:T(1,128)S(1)}, u32[]{:S(2)}, u32[]{:S(2)}) collective-permute-start(f32[1,4352]{1,0:T(1,128)S(1)} %broadcast_in_dim.26), channel_id=1, source_target_pairs={{0,16},{2,18},{4,20},{6,22},{8,24},{10,26},{12,28},{14,30},{16,0},... | collective-permute-start | bytes 52232 | tf_op jit(solution)/shard_map/ppermute | solution.py:239
  45.9 2.2 %collective-permute-done.1 = f32[1,4352]{1,0:T(1,128)S(1)} collective-permute-done((f32[1,4352]{1,0:T(1,128)S(1)}, f32[1,4352]{1,0:T(1,128)S(1)}, u32[]{:S(2)}, u32[]{:S(2)}) %collective-permute-start.1) | collective-permute-done | bytes 17440 | tf_op jit(solution)/shard_map/ppermute | solution.py:239
  48.1 1.5 collective-permute-start.2
  49.6 2.5 %collective-permute-done.2 = f32[2,4352]{1,0:T(2,128)S(1)} collective-permute-done((f32[2,4352]{1,0:T(2,128)S(1)}, f32[2,4352]{1,0:T(2,128)S(1)}, u32[]{:S(2)}, u32[]{:S(2)}) %collective-permute-start.2) | collective-permute-done | bytes 34848 | tf_op jit(solution)/shard_map/ppermute | solution.py:239
  52.2 1.8 %collective-permute-start.3 = (f32[4,4352]{1,0:T(4,128)S(1)}, f32[4,4352]{1,0:T(4,128)S(1)}, u32[]{:S(2)}, u32[]{:S(2)}) collective-permute-start(f32[4,4352]{1,0:T(4,128)S(1)} %pad_maximum_fusion.3), channel_id=1, source_target_pairs={{0,4},{2,6},{4,0},{6,2},{8,12},{10,14},{12,8},{14,10},{16,20},{18,... | collective-permute-start | bytes 208904 | tf_op jit(solution)/shard_map/ppermute | solution.py:239
  54.0 2.5 %collective-permute-done.3 = f32[4,4352]{1,0:T(4,128)S(1)} collective-permute-done((f32[4,4352]{1,0:T(4,128)S(1)}, f32[4,4352]{1,0:T(4,128)S(1)}, u32[]{:S(2)}, u32[]{:S(2)}) %collective-permute-start.3) | collective-permute-done | bytes 69664 | tf_op jit(solution)/shard_map/ppermute | solution.py:239
  56.7 1.3 collective-permute-done.4
  58.8 30.4 %code_mass.1 = (f32[1,4096]{1,0:T(1,128)}, f32[8,4096]{1,0:T(8,128)}) custom-call(s32[1]{0:T(128)} %bitcast.me_ref, bf16[4096,256]{1,0:T(8,128)(2,1)} %all-gather.2.cloned.1.call-done.rows_ref, bf16[65536,256]{1,0:T(8,128)(2,1)} %codes_ref.7, f32[16,256]{1,0:T(8,128)} %slice.27.lse_ref), custom_call_target="tpu_custom_call" | custom-call | tf_op jit(solution)/shard_map/code_mass/pallas_call | solution.py:113
  89.1 0.9 reduce_sum.28
  90.0 1.5 collective-permute-start.5
  91.5 2.4 %collective-permute-done.5 = f32[4096]{0:T(1024)S(1)} collective-permute-done((f32[4096]{0:T(1024)S(1)}, f32[4096]{0:T(1024)S(1)}, u32[]{:S(2)}, u32[]{:S(2)}) %collective-permute-start.5) | collective-permute-done | bytes 16416 | tf_op jit(solution)/shard_map/ppermute | solution.py:239
  93.9 0.7 pad_maximum_fusion.6
  94.6 2.9 %collective-permute-start.6 = (f32[1,8192]{1,0:T(1,128)S(1)}, f32[1,8192]{1,0:T(1,128)S(1)}, u32[]{:S(2)}, u32[]{:S(2)}) collective-permute-start(f32[1,8192]{1,0:T(1,128)S(1)} %bitcast.8), channel_id=1, source_target_pairs={{0,16},{2,18},{4,20},{6,22},{8,24},{10,26},{12,28},{14,30},{16,0},... | collective-permute-start | bytes 98312 | tf_op jit(solution)/shard_map/ppermute | solution.py:239
  97.5 2.1 %collective-permute-done.6 = f32[1,8192]{1,0:T(1,128)S(1)} collective-permute-done((f32[1,8192]{1,0:T(1,128)S(1)}, f32[1,8192]{1,0:T(1,128)S(1)}, u32[]{:S(2)}, u32[]{:S(2)}) %collective-permute-start.6) | collective-permute-done | bytes 32800 | tf_op jit(solution)/shard_map/ppermute | solution.py:239
  99.6 1.9 %collective-permute-start.7 = (f32[2,8192]{1,0:T(2,128)S(1)}, f32[2,8192]{1,0:T(2,128)S(1)}, u32[]{:S(2)}, u32[]{:S(2)}) collective-permute-start(f32[2,8192]{1,0:T(2,128)S(1)} %pad_maximum_fusion.4), channel_id=1, source_target_pairs={{0,8},{2,10},{4,12},{6,14},{8,0},{10,2},{12,4},{14,6},{16,24},{18,... | collective-permute-start | bytes 196616 | tf_op jit(solution)/shard_map/ppermute | solution.py:239
  101.5 2.4 %collective-permute-done.7 = f32[2,8192]{1,0:T(2,128)S(1)} collective-permute-done((f32[2,8192]{1,0:T(2,128)S(1)}, f32[2,8192]{1,0:T(2,128)S(1)}, u32[]{:S(2)}, u32[]{:S(2)}) %collective-permute-start.7) | collective-permute-done | bytes 65568 | tf_op jit(solution)/shard_map/ppermute | solution.py:239
  104.1 1.7 collective-permute-start.8
  105.7 3.4 %collective-permute-done.8 = f32[4,8192]{1,0:T(4,128)S(1)} collective-permute-done((f32[4,8192]{1,0:T(4,128)S(1)}, f32[4,8192]{1,0:T(4,128)S(1)}, u32[]{:S(2)}, u32[]{:S(2)}) %collective-permute-start.8) | collective-permute-done | bytes 131104 | tf_op jit(solution)/shard_map/ppermute | solution.py:239
  109.3 1.0 copy.5.squares_ref
  111.1 1.0 broadcast_in_dim.30.log_ref
  112.2 0.8 broadcast_in_dim.12.lse_ref
  112.9 0.8 broadcast_in_dim.28.shift_ref
  113.7 26.7 %grad_rows.1 = f32[256,256]{1,0:T(8,128)} custom-call(s32[1]{0:T(128)} %bitcast.me_ref, bf16[256,256]{1,0:T(8,128)(2,1)} %encoded_ref.1, bf16[65536,256]{1,0:T(8,128)(2,1)} %codes_ref.7, f32[256,128]{1,0:T(8,128)} %broadcast_in_dim.12.lse_ref, f32[256,128]{1,0:T(8,128)} %broadcast_in_dim.28.shift_ref, f32[16,1,4096]{2,1,0:T(1,128)} %copy.5.squares_ref, ...), custom_call_target="tpu_custom_call" | custom-call | tf_op jit(solution)/shard_map/grad_rows/pallas_call | solution.py:171
  140.3 1.3 collective-permute-start.10
  141.6 31.0 %grad_codes.1 = f32[4096,256]{1,0:T(8,128)} custom-call(s32[1]{0:T(128)} %bitcast.me_ref, bf16[4096,256]{1,0:T(8,128)(2,1)} %all-gather.2.cloned.1.call-done.rows_ref, bf16[65536,256]{1,0:T(8,128)(2,1)} %codes_ref.7, f32[16,256]{1,0:T(8,128)} %slice.27.lse_ref, f32[1,4096]{1,0:T(1,128)} %bitcast.14, f32[1,4096]{1,0:T(1,128)} %get-tuple-element.8.log_ref), custom_call_target="tpu_custom_call" | custom-call | tf_op jit(solution)/shard_map/grad_codes/pallas_call | solution.py:218
  172.6 0.7 add.34
  (29 shorter events, 2.9 us)
Async XLA Ops:
  7.2 51.6 %all-gather.2.cloned.1.call-start = ((), (), s32[]{:S(2)}) async-start(), calls=%async_computation | async-start | bytes 2228224 | tf_op jit(solution)/shard_map/all_gather | solution.py:267
  37.3 5.2 %collective-permute-start = (f32[2,256]{1,0:T(2,128)S(1)}, f32[2,256]{1,0:T(2,128)S(1)}, u32[]{:S(2)}, u32[]{:S(2)}) collective-permute-start(f32[2,256]{1,0:T(2,128)S(1)} %pad_maximum_fusion.8), channel_id=1, source_target_pairs={{0,1},{1,0},{2,3},{3,2},{4,5},{5,4},{6,7},{7,6},{8,9},{9,8},{10,11... | collective-permute-start | bytes 6152 | tf_op jit(solution)/shard_map/ppermute | solution.py:239
  43.2 4.8 %collective-permute-start.1 = (f32[1,4352]{1,0:T(1,128)S(1)}, f32[1,4352]{1,0:T(1,128)S(1)}, u32[]{:S(2)}, u32[]{:S(2)}) collective-permute-start(f32[1,4352]{1,0:T(1,128)S(1)} %broadcast_in_dim.26), channel_id=1, source_target_pairs={{0,16},{2,18},{4,20},{6,22},{8,24},{10,26},{12,28},{14,30},{16,0},... | collective-permute-start | bytes 52232 | tf_op jit(solution)/shard_map/ppermute | solution.py:239
  48.1 4.0 %collective-permute-start.2 = (f32[2,4352]{1,0:T(2,128)S(1)}, f32[2,4352]{1,0:T(2,128)S(1)}, u32[]{:S(2)}, u32[]{:S(2)}) collective-permute-start(f32[2,4352]{1,0:T(2,128)S(1)} %pad_maximum_fusion.5), channel_id=1, source_target_pairs={{0,8},{2,10},{4,12},{6,14},{8,0},{10,2},{12,4},{14,6},{16,24},{18,... | collective-permute-start | bytes 104456 | tf_op jit(solution)/shard_map/ppermute | solution.py:239
  52.2 4.4 %collective-permute-start.3 = (f32[4,4352]{1,0:T(4,128)S(1)}, f32[4,4352]{1,0:T(4,128)S(1)}, u32[]{:S(2)}, u32[]{:S(2)}) collective-permute-start(f32[4,4352]{1,0:T(4,128)S(1)} %pad_maximum_fusion.3), channel_id=1, source_target_pairs={{0,4},{2,6},{4,0},{6,2},{8,12},{10,14},{12,8},{14,10},{16,20},{18,... | collective-permute-start | bytes 208904 | tf_op jit(solution)/shard_map/ppermute | solution.py:239
  56.6 1.4 collective-permute-start.4
  90.0 3.8 %collective-permute-start.5 = (f32[4096]{0:T(1024)S(1)}, f32[4096]{0:T(1024)S(1)}, u32[]{:S(2)}, u32[]{:S(2)}) collective-permute-start(f32[4096]{0:T(1024)S(1)} %reduce_sum.28), channel_id=1, source_target_pairs={{0,1},{1,0},{2,3},{3,2},{4,5},{5,4},{6,7},{7,6},{8,9},{9,8},{10,11... | collective-permute-start | bytes 49160 | tf_op jit(solution)/shard_map/ppermute | solution.py:239
  94.6 5.0 %collective-permute-start.6 = (f32[1,8192]{1,0:T(1,128)S(1)}, f32[1,8192]{1,0:T(1,128)S(1)}, u32[]{:S(2)}, u32[]{:S(2)}) collective-permute-start(f32[1,8192]{1,0:T(1,128)S(1)} %bitcast.8), channel_id=1, source_target_pairs={{0,16},{2,18},{4,20},{6,22},{8,24},{10,26},{12,28},{14,30},{16,0},... | collective-permute-start | bytes 98312 | tf_op jit(solution)/shard_map/ppermute | solution.py:239
  99.6 4.3 %collective-permute-start.7 = (f32[2,8192]{1,0:T(2,128)S(1)}, f32[2,8192]{1,0:T(2,128)S(1)}, u32[]{:S(2)}, u32[]{:S(2)}) collective-permute-start(f32[2,8192]{1,0:T(2,128)S(1)} %pad_maximum_fusion.4), channel_id=1, source_target_pairs={{0,8},{2,10},{4,12},{6,14},{8,0},{10,2},{12,4},{14,6},{16,24},{18,... | collective-permute-start | bytes 196616 | tf_op jit(solution)/shard_map/ppermute | solution.py:239
  104.1 5.0 %collective-permute-start.8 = (f32[4,8192]{1,0:T(4,128)S(1)}, f32[4,8192]{1,0:T(4,128)S(1)}, u32[]{:S(2)}, u32[]{:S(2)}) collective-permute-start(f32[4,8192]{1,0:T(4,128)S(1)} %pad_maximum_fusion.2), channel_id=1, source_target_pairs={{0,4},{2,6},{4,0},{6,2},{8,12},{10,14},{12,8},{14,10},{16,20},{18,... | collective-permute-start | bytes 393224 | tf_op jit(solution)/shard_map/ppermute | solution.py:239
  109.2 1.6 collective-permute-start.9
  112.1 28.3 %copy-start.1 = (f32[4096]{0:T(1024)}, f32[4096]{0:T(1024)S(1)}, u32[]{:S(2)}) copy-start(f32[4096]{0:T(1024)S(1)} %broadcast_multiply_fusion) | copy-start | bytes 49156
  140.3 32.3 %collective-permute-start.10 = (f32[256,256]{1,0:T(8,128)}, f32[256,256]{1,0:T(8,128)S(1)}, u32[]{:S(2)}, u32[]{:S(2)}) collective-permute-start(f32[256,256]{1,0:T(8,128)} %grad_rows.1), channel_id=1, source_target_pairs={{0,1},{1,0},{2,3},{3,2},{4,5},{5,4},{6,7},{7,6},{8,9},{9,8},{10,11... | collective-permute-start | bytes 786440 | tf_op jit(solution)/shard_map/ppermute | solution.py:239
  141.6 31.0 %copy-start = (f32[256,256]{1,0:T(8,128)S(1)}, f32[256,256]{1,0:T(8,128)}, u32[]{:S(2)}) copy-start(f32[256,256]{1,0:T(8,128)} %grad_rows.1) | copy-start | bytes 786436
Sparse Core Ops, SparseCore 0:
  10.2 43.9 all-gather.1

commit v2 on v1

v2 whole, which is shorter than its diff:
```python
import math

import jax
import jax.numpy as jnp
from jax import lax
from jax.experimental import pallas as pl
from jax.experimental.pallas import tpu as pltpu
from jax.sharding import PartitionSpec as P

LOG2E = math.log2(math.e)
LN2 = math.log(2.0)
LOG2LN2 = math.log2(LN2)
LANES = 128
PARAMS = pltpu.CompilerParams(vmem_limit_bytes=56 * 2**20)
NT = (((1,), (1,)), ((), ()))


def squared(code_rows):
    values = code_rows.astype(jnp.float32)
    return jnp.sum(values * values, axis=1, keepdims=True)


def column_to_row(column):
    wide = jnp.broadcast_to(column, (column.shape[0], LANES))
    return jnp.transpose(wide)[0:1, :]


def row_to_columns(row):
    return jnp.transpose(jnp.broadcast_to(row, (LANES, row.shape[1])))


def stats_call(encoded, codebook, state, first, last):
    rows, features = encoded.shape
    block = math.gcd(math.gcd(first, last), 8192)
    chunk = math.gcd(block, 256)
    done = last == codebook.shape[0]

    def kernel(encoded_ref, codes_ref, state_ref, out_ref, turned, top, total):
        step = pl.program_id(0)

        @pl.when(step == 0)
        def _():
            turned[...] = jnp.transpose(encoded_ref[...]) * jnp.bfloat16(2.0)
            top[...] = state_ref[0]
            total[...] = state_ref[1]

        run_max, run_sum = top[...], total[...]
        for k in range(block // chunk):
            code_rows = codes_ref[k * chunk : (k + 1) * chunk, :]
            scores = jnp.dot(code_rows, turned[...], preferred_element_type=jnp.float32)
            logits = ((scores - squared(code_rows)) * (0.5 * LOG2E)).reshape(chunk // 8, 8, rows)
            new_max = jnp.maximum(run_max, jnp.max(logits, axis=0))
            powers = jnp.exp2(logits - new_max[None])
            run_sum = run_sum * jnp.exp2(run_max - new_max) + jnp.sum(powers, axis=0)
            run_max = new_max
        top[...] = run_max
        total[...] = run_sum

        @pl.when(step == pl.num_programs(0) - 1)
        def _():
            if done:
                row_max = jnp.max(run_max, axis=0, keepdims=True)
                out_ref[0:1, :] = row_max
                out_ref[1:2, :] = jnp.sum(run_sum * jnp.exp2(run_max - row_max), axis=0, keepdims=True)
            else:
                out_ref[0] = run_max
                out_ref[1] = run_sum

    shape = (2, rows) if done else (2, 8, rows)
    return pl.pallas_call(
        kernel,
        grid=((last - first) // block,),
        in_specs=[
            pl.BlockSpec((rows, features), lambda i: (0, 0)),
            pl.BlockSpec((block, features), lambda i: (first // block + i, 0)),
            pl.BlockSpec((2, 8, rows), lambda i: (0, 0, 0)),
        ],
        out_specs=pl.BlockSpec(shape, lambda i: (0,) * len(shape)),
        out_shape=jax.ShapeDtypeStruct(shape, jnp.float32),
        scratch_shapes=[pltpu.VMEM((features, rows), jnp.bfloat16)] + [pltpu.VMEM((8, rows), jnp.float32)] * 2,
        compiler_params=PARAMS,
        name="row_stats",
    )(encoded, codebook, state)


def place_of(offset, count):
    bits = count.bit_length() - 1
    return sum(((offset >> b) & 1) << (bits - 1 - b) for b in range(bits))


def piece_of(place, rows):
    piece = place.bit_length()
    return piece, (place - (1 << (piece - 1) if piece else 0)) * rows


def mass_call(me, pieces, codebook, all_lse, devices, own):
    rows, features = pieces[0].shape
    total_rows = rows * devices
    block = math.gcd(own, 512)
    steps = own // block

    def kernel(me_ref, codes_ref, lse_ref, *refs):
        row_refs, (log_ref, squares_ref, cross_ref, cross, logits_scr) = refs[: len(pieces)], refs[len(pieces) :]
        step = pl.program_id(0)

        @pl.when(step == 0)
        def _():
            cross[...] = jnp.zeros(cross.shape, jnp.float32)

        code_rows = codes_ref[...]
        squares = squared(code_rows)
        half = jnp.broadcast_to(squares, (block, LANES))
        doubled = code_rows * jnp.bfloat16(2.0)
        mass = jnp.zeros((block, LANES), jnp.float32)
        for p in range(devices):
            piece, start = piece_of(p, rows)
            row_block = row_refs[piece][start : start + rows, :]
            scores = lax.dot_general(doubled, row_block, NT, preferred_element_type=jnp.float32)
            for q in range(rows // LANES):
                lane = slice(q * LANES, (q + 1) * LANES)
                logits = (scores[:, lane] - half) * (0.5 * LOG2E) - lse_ref[p, :, lane]
                logits_scr[:, p * rows + q * LANES : p * rows + (q + 1) * LANES] = logits
                mass = mass + jnp.exp2(logits)
        log_mass = jnp.log2(jnp.sum(mass, axis=1, keepdims=True) * (1.0 / (LN2 * total_rows)))
        log_ref[0] = column_to_row(log_mass)
        squares_ref[0] = column_to_row(squares) * (0.5 * LOG2E)
        log_wide = jnp.broadcast_to(log_mass, (block, LANES))
        for q in range(total_rows // LANES):
            there = slice(q * LANES, (q + 1) * LANES)
            logits = logits_scr[:, there]
            terms = jnp.exp2(logits) * (log_wide - logits)
            cross[:, there] += jnp.sum(terms.reshape(block // 8, 8, LANES), axis=0)

        @pl.when(step == pl.num_programs(0) - 1)
        def _():
            for p in range(devices):
                there = pl.ds(pl.multiple_of((me_ref[0] ^ place_of(p, devices)) * rows, rows), rows)
                cross_ref[:, there] = jnp.sum(cross[:, p * rows : (p + 1) * rows], axis=0, keepdims=True)

    return pl.pallas_call(
        kernel,
        grid_spec=pltpu.PrefetchScalarGridSpec(
            num_scalar_prefetch=1,
            grid=(steps,),
            in_specs=[
                pl.BlockSpec((block, features), lambda i, me: (me[0] * steps + i, 0)),
                pl.BlockSpec((devices, 1, rows), lambda i, me: (0, 0, 0)),
            ]
            + [pl.BlockSpec(piece.shape, lambda i, me: (0, 0)) for piece in pieces],
            out_specs=[
                pl.BlockSpec((1, 1, block), lambda i, me: (0, 0, i)),
                pl.BlockSpec((1, 1, block), lambda i, me: (0, 0, i)),
                pl.BlockSpec((1, total_rows), lambda i, me: (0, 0)),
            ],
            scratch_shapes=[
                pltpu.VMEM((8, total_rows), jnp.float32),
                pltpu.VMEM((block, total_rows), jnp.float32),
            ],
        ),
        out_shape=[
            jax.ShapeDtypeStruct((1, 1, own), jnp.float32),
            jax.ShapeDtypeStruct((1, 1, own), jnp.float32),
            jax.ShapeDtypeStruct((1, total_rows), jnp.float32),
        ],
        compiler_params=PARAMS,
        name="code_mass",
    )(me, codebook, all_lse, *pieces)


def rows_call(me, encoded, codebook, row_lse, shift, gathered, devices, own):
    rows, features = encoded.shape
    codes = codebook.shape[0]
    block = math.gcd(own, 4096)
    per_device = own // block
    chunk = math.gcd(block, 512)

    def kernel(me_ref, encoded_ref, codes_ref, lse_ref, shift_ref, log_ref, squares_ref, out_ref, lse_wide, shift_wide):
        @pl.when(pl.program_id(0) == 0)
        def _():
            out_ref[...] = jnp.zeros(out_ref.shape, jnp.float32)
            mine = pl.ds(pl.multiple_of(me_ref[0] * rows, rows), rows)
            lse_wide[...] = row_to_columns(lse_ref[...])
            shift_wide[...] = row_to_columns(shift_ref[:, mine])

        encoded_here = encoded_ref[...]
        total = out_ref[...]
        for k in range(block // chunk):
            part = slice(k * chunk, (k + 1) * chunk)
            code_rows = codes_ref[part, :]
            scores = lax.dot_general(encoded_here, code_rows, NT, preferred_element_type=jnp.float32)
            log_mass = log_ref[0, :, part]
            squares = squares_ref[0, :, part]
            tiles = []
            for q in range(chunk // LANES):
                lane = slice(q * LANES, (q + 1) * LANES)
                logits = scores[:, lane] * LOG2E - squares[:, lane] - lse_wide[...]
                tile = jnp.exp2(logits) * (log_mass[:, lane] - logits + shift_wide[...])
                tiles.append(tile.astype(jnp.bfloat16))
            grad_tile = jnp.concatenate(tiles, axis=1)
            total = total + jnp.dot(grad_tile, code_rows, preferred_element_type=jnp.float32)
        out_ref[...] = total

    def log_map(i, me):
        return (place_of(me[0] ^ (i // per_device), devices), 0, i % per_device)

    def squares_map(i, me):
        return (place_of(me[0] ^ (i // per_device), devices), 0, per_device + i % per_device)

    return pl.pallas_call(
        kernel,
        grid_spec=pltpu.PrefetchScalarGridSpec(
            num_scalar_prefetch=1,
            grid=(codes // block,),
            in_specs=[
                pl.BlockSpec((rows, features), lambda i, me: (0, 0)),
                pl.BlockSpec((block, features), lambda i, me: (i, 0)),
                pl.BlockSpec(row_lse.shape, lambda i, me: (0, 0)),
                pl.BlockSpec(shift.shape, lambda i, me: (0, 0)),
                pl.BlockSpec((1, 1, block), log_map),
                pl.BlockSpec((1, 1, block), squares_map),
            ],
            out_specs=pl.BlockSpec((rows, features), lambda i, me: (0, 0)),
            scratch_shapes=[pltpu.VMEM((rows, LANES), jnp.float32)] * 2,
        ),
        out_shape=jax.ShapeDtypeStruct((rows, features), jnp.float32),
        compiler_params=PARAMS,
        name="grad_rows",
    )(me, encoded, codebook, row_lse, shift, gathered, gathered)


def codes_call(me, pieces, codebook, all_lse, shift, log_mass, squares, devices, own, CHAINS=1, BLOCK=512):
    rows, features = pieces[0].shape
    block = math.gcd(own, BLOCK)
    blocks = own // block

    def kernel(me_ref, codes_ref, lse_ref, shift_ref, log_ref, squares_ref, *refs):
        row_refs, out_ref = refs[:-1], refs[-1]
        log_mass = row_to_columns(log_ref[0])
        half = row_to_columns(squares_ref[0])
        code_rows = codes_ref[...]
        totals = [jnp.zeros((block, features), jnp.float32)] * CHAINS
        sums = jnp.zeros((block, LANES), jnp.float32)
        for p in range(devices):
            piece, start = piece_of(p, rows)
            row_block = row_refs[piece][start : start + rows, :]
            scores = lax.dot_general(code_rows, row_block, NT, preferred_element_type=jnp.float32)
            there = pl.ds(pl.multiple_of((me_ref[0] ^ place_of(p, devices)) * rows, rows), rows)
            shift_here = shift_ref[:, there]
            tiles = []
            for q in range(rows // LANES):
                lane = slice(q * LANES, (q + 1) * LANES)
                logits = scores[:, lane] * LOG2E - half - lse_ref[p, :, lane]
                tile = jnp.exp2(logits) * (log_mass - logits + shift_here[:, lane])
                sums = sums + tile
                tiles.append(tile.astype(jnp.bfloat16))
            grad_tile = jnp.concatenate(tiles, axis=1)
            totals[p % CHAINS] = totals[p % CHAINS] + jnp.dot(
                grad_tile, row_block, preferred_element_type=jnp.float32
            )
        code_sums = jnp.sum(sums, axis=1, keepdims=True)
        out_ref[...] = sum(totals) - code_sums * code_rows.astype(jnp.float32)

    return pl.pallas_call(
        kernel,
        grid_spec=pltpu.PrefetchScalarGridSpec(
            num_scalar_prefetch=1,
            grid=(blocks,),
            in_specs=[
                pl.BlockSpec((block, features), lambda i, me: (me[0] * blocks + i, 0)),
                pl.BlockSpec((devices, 1, rows), lambda i, me: (0, 0, 0)),
                pl.BlockSpec((1, rows * devices), lambda i, me: (0, 0)),
                pl.BlockSpec((1, 1, block), lambda i, me: (0, 0, i)),
                pl.BlockSpec((1, 1, block), lambda i, me: (0, 0, i)),
            ]
            + [pl.BlockSpec(piece.shape, lambda i, me: (0, 0)) for piece in pieces],
            out_specs=pl.BlockSpec((block, features), lambda i, me: (i, 0)),
        ),
        out_shape=jax.ShapeDtypeStruct((own, features), jnp.float32),
        compiler_params=PARAMS,
        name="grad_codes",
    )(me, codebook, all_lse, shift, log_mass, squares, *pieces)


def from_xor(values, axis, offset):
    return lax.ppermute(values, axis, [(i, i ^ offset) for i in range(lax.axis_size(axis))])


def xor_gather(held, axis):
    offset = lax.axis_size(axis) // 2
    while offset:
        held = jnp.concatenate([held, from_xor(held, axis, offset)], axis=0)
        offset //= 2
    return held


def xor_sum(values, axis):
    offset = lax.axis_size(axis) // 2
    while offset:
        values = values + from_xor(values, axis, offset)
        offset //= 2
    return values


def body(encoded, codebook):
    rows, features = encoded.shape
    codes = codebook.shape[0]
    devices = lax.axis_size("dp")
    own = codes // devices
    me = lax.axis_index("dp").astype(jnp.int32).reshape(1)
    offsets = [devices >> (k + 1) for k in range(devices.bit_length() - 1)]

    pieces = [encoded]

    def gather_more(after):
        if len(pieces) > len(offsets):
            return after
        held, after = lax.optimization_barrier((tuple(pieces), after))
        pieces[:] = held
        joined = lax.optimization_barrier(jnp.concatenate(pieces, axis=0)) if len(pieces) > 1 else encoded
        pieces.append(from_xor(joined, "dp", offsets[len(pieces) - 1]))
        return after

    state = jnp.stack([jnp.full((8, rows), -3e38, jnp.float32), jnp.zeros((8, rows), jnp.float32)])
    state = gather_more(state)
    state = stats_call(encoded, codebook, state, 0, codes // 2)
    state = gather_more(state)
    stats = stats_call(encoded, codebook, state, codes // 2, codes)
    stats = gather_more(stats)
    offset = lax.axis_size("code") // 2
    while offset:
        other = from_xor(stats, "code", offset)
        top = jnp.maximum(stats[0:1], other[0:1])
        total = stats[1:2] * jnp.exp2(stats[0:1] - top) + other[1:2] * jnp.exp2(other[0:1] - top)
        stats = jnp.concatenate([top, total], axis=0)
        offset //= 2
    row_lse = stats[0:1] + jnp.log2(stats[1:2]) - LOG2LN2
    all_lse = lax.optimization_barrier(row_lse[None])
    for k, offset in enumerate(offsets):
        all_lse = jnp.concatenate([all_lse, from_xor(all_lse, "dp", offset)], axis=0)
        if k:
            all_lse = gather_more(all_lse)

    log_mass, squares, cross = mass_call(me, pieces, codebook, all_lse, devices, own)
    cross = xor_sum(cross, "code")
    message = jnp.concatenate([log_mass, squares, cross[None]], axis=2)
    gathered = xor_gather(lax.optimization_barrier(message), "dp")
    shift = jnp.sum(gathered[:, :, 2 * own :], axis=0) * (-1.0 / LN2)

    local_rows = rows_call(me, encoded, codebook, row_lse, shift, gathered, devices, own)
    grad_codes = codes_call(me, pieces, codebook, all_lse, shift, log_mass, squares, devices, own)
    grad_rows = xor_sum(local_rows, "code")
    return grad_rows, grad_codes


def solution(mesh):
    placed = (P("dp", None), P("code", None))
    return jax.shard_map(
        body,
        mesh=mesh,
        in_specs=placed,
        out_specs=(P("dp", None), P(("code", "dp"), None)),
        check_vma=False,
    )
```

time: 181 us -> 164 us (0.906)
  between operations: 14.1 us -> 0.85 us
  waiting for transfers between devices: 20 us -> 27.7 us
  Pallas kernels: 115 us -> 109 us
  local copies, waits for them, and re-layouts: 6.18 us -> 1.15 us
  other arithmetic: 6.51 us -> 4.69 us
    ppermute x11 -> x15, waiting for transfers between devices: 19.3 us -> 27.7 us  [from_xor(): lax.ppermute(values, axis, [(i, i ^ offset) for i in range(lax.axis_size(...]
    pallas_call x1, Pallas kernels: 30.4 us -> 25.8 us  [mass_call(): pl.pallas_call(kernel, grid_spec=pltpu.PrefetchScalarGridSpec(num_scalar_...]
    broadcast_in_dim x6 -> x0, local copies, waits for them, and re-layouts: 3.49 us -> none  [the longest x2 0.99 us: body(): all_lse, all_squares = (gathered[:, :rows], gathered[:, None, rows:])]
    reduce_sum x2 -> x1, other arithmetic: 3.15 us -> 0.12 us  [body(): shift = jnp.sum(gathered[:, :, 2 * own:], axis=0) * (-1.0 / LN2)]
    pallas_call x1, Pallas kernels: 31 us -> 28.6 us  [codes_call(): pl.pallas_call(kernel, grid_spec=pltpu.PrefetchScalarGridSpec(num_scalar_...]
    pallas_call x1 -> x2, Pallas kernels: 27 us -> 28.3 us  [stats_call(): pl.pallas_call(kernel, grid=((last - first) // block,), in_specs=[pl.Bloc...]
    ppermute x11 -> x15, starting transfers between devices: 18.3 us -> 19.2 us  [from_xor(): lax.ppermute(values, axis, [(i, i ^ offset) for i in range(lax.axis_size(...]
  transfers between devices with their start and end apart: 12 -> 15, of which waited for: 9 -> 10; matrix products, arithmetic and copies ran while one was open for 4% -> 1% of each run, Pallas kernels for 32% -> 35%
where the time goes in v2:
time: 164 us; the launch traced here: 163 us
  Pallas kernels  109 us (66%)
  waiting for transfers between devices  27.7 us (17%)
  starting transfers between devices  19.2 us (12%)
  other arithmetic  4.69 us (3%)
    pallas_call x1, Pallas kernels, codes_call(): pl.pallas_call(kernel, grid_spec=pltpu.PrefetchScalarGridSpec(num_scalar_...  28.6 us
    pallas_call x2, Pallas kernels, stats_call(): pl.pallas_call(kernel, grid=((last - first) // block,), in_specs=[pl.Bloc...  28.3 us
    ppermute x15, waiting for transfers between devices, from_xor(): lax.ppermute(values, axis, [(i, i ^ offset) for i in range(lax.axis_size(...  27.7 us
    pallas_call x1, Pallas kernels, rows_call(): pl.pallas_call(kernel, grid_spec=pltpu.PrefetchScalarGridSpec(num_scalar_...  26.7 us
    pallas_call x1, Pallas kernels, mass_call(): pl.pallas_call(kernel, grid_spec=pltpu.PrefetchScalarGridSpec(num_scalar_...  25.8 us
    ppermute x15, starting transfers between devices, from_xor(): lax.ppermute(values, axis, [(i, i ^ offset) for i in range(lax.axis_size(...  19.2 us
  transfers between devices with their start and end apart: 15, of which 10 were waited for; matrix products, arithmetic and copies ran while one was open for 1% of the time, Pallas kernels for 35%

profile of v2, /device:TPU:0, one launch (start us, length us, event | category | flops | bytes accessed | tf_op | source)
XLA Modules:
  0.0 163.0 jit_solution(7773202758124590178)
XLA Ops:
  0.6 4.1 %collective-permute-start = (bf16[256,256]{1,0:T(8,128)(2,1)}, bf16[256,256]{1,0:T(8,128)(2,1)S(1)}, u32[]{:S(2)}, u32[]{:S(2)}) collective-permute-start(bf16[256,256]{1,0:T(8,128)(2,1)} %refs_0_.1), channel_id=1, source_target_pairs={{0,16},{2,18},{4,20},{6,22},{8,24},{10,26},{12,28},{14,30},{16,0},... | collective-permute-start | bytes 393224 | tf_op jit(solution)/shard_map/ppermute | solution.py:285
  4.7 14.2 %row_stats.2.state_ref = f32[2,8,256]{2,1,0:T(8,128)} custom-call(bf16[256,256]{1,0:T(8,128)(2,1)} %refs_0_.1, bf16[65536,256]{1,0:T(8,128)(2,1)} %codes_ref.9, f32[2,8,256]{2,1,0:T(8,128)} %constant.5.clone.1.state_ref), custom_call_target="tpu_custom_call" | custom-call | tf_op jit(solution)/shard_map/row_stats/pallas_call | solution.py:70
  19.0 1.6 %collective-permute-start.1 = (bf16[512,256]{1,0:T(8,128)(2,1)S(1)}, bf16[512,256]{1,0:T(8,128)(2,1)S(1)}, u32[]{:S(2)}, u32[]{:S(2)}) collective-permute-start(bf16[512,256]{1,0:T(8,128)(2,1)S(1)} %pad_maximum_fusion.3), channel_id=1, source_target_pairs={{0,8},{2,10},{4,12},{6,14},{8,0},{10,2},{12,4},{14,6},{16,24},{18,... | collective-permute-start | bytes 786440 | tf_op jit(solution)/shard_map/ppermute | solution.py:285
  20.6 14.2 %row_stats.3 = f32[2,256]{1,0:T(2,128)} custom-call(bf16[256,256]{1,0:T(8,128)(2,1)} %refs_0_.1, bf16[65536,256]{1,0:T(8,128)(2,1)} %codes_ref.9, f32[2,8,256]{2,1,0:T(8,128)} %row_stats.2.state_ref), custom_call_target="tpu_custom_call" | custom-call | tf_op jit(solution)/shard_map/row_stats/pallas_call | solution.py:70
  34.8 1.6 collective-permute-start.3
  36.4 1.5 collective-permute-start.2
  37.9 2.3 %collective-permute-done.2 = f32[2,256]{1,0:T(2,128)S(1)} collective-permute-done((f32[2,256]{1,0:T(2,128)}, f32[2,256]{1,0:T(2,128)S(1)}, u32[]{:S(2)}, u32[]{:S(2)}) %collective-permute-start.2) | collective-permute-done | bytes 2080 | tf_op jit(solution)/shard_map/ppermute | solution.py:285
  40.2 0.8 add_add_fusion.lse_ref
  41.0 1.5 collective-permute-start.4
  42.5 3.1 %collective-permute-done.4 = f32[1,1,256]{2,1,0:T(1,128)S(1)} collective-permute-done((f32[1,1,256]{2,1,0:T(1,128)S(1)}, f32[1,1,256]{2,1,0:T(1,128)S(1)}, u32[]{:S(2)}, u32[]{:S(2)}) %collective-permute-start.4) | collective-permute-done | bytes 1056 | tf_op jit(solution)/shard_map/ppermute | solution.py:285
  45.5 1.5 collective-permute-start.5
  47.0 2.1 %collective-permute-done.5 = f32[2,1,256]{2,1,0:T(1,128)S(1)} collective-permute-done((f32[2,1,256]{2,1,0:T(1,128)S(1)}, f32[2,1,256]{2,1,0:T(1,128)S(1)}, u32[]{:S(2)}, u32[]{:S(2)}) %collective-permute-start.5) | collective-permute-done | bytes 2080 | tf_op jit(solution)/shard_map/ppermute | solution.py:285
  49.3 0.6 collective-permute-start.6
  49.9 3.1 %collective-permute-done.6 = f32[4,1,256]{2,1,0:T(1,128)S(1)} collective-permute-done((f32[4,1,256]{2,1,0:T(1,128)S(1)}, f32[4,1,256]{2,1,0:T(1,128)S(1)}, u32[]{:S(2)}, u32[]{:S(2)}) %collective-permute-start.6) | collective-permute-done | bytes 4128 | tf_op jit(solution)/shard_map/ppermute | solution.py:285
  53.1 1.1 collective-permute-done.7
  55.3 25.8 %code_mass.1 = (f32[1,1,4096]{2,1,0:T(1,128)}, f32[1,1,4096]{2,1,0:T(1,128)}, f32[1,4096]{1,0:T(1,128)}) custom-call(s32[1]{0:T(128)} %bitcast.me_ref, bf16[65536,256]{1,0:T(8,128)(2,1)} %codes_ref.9, f32[16,1,256]{2,1,0:T(1,128)} %copy-done.8, bf16[256,256]{1,0:T(8,128)(2,1)} %refs_0_.1, bf16[256,256]{1,0:T(8,128)(2,1)} %copy-done.6, ...), custom_call_target="tpu_custom_call" | custom-call | tf_op jit(solution)/shard_map/code_mass/pallas_call | solution.py:140
  81.1 1.6 collective-permute-start.9
  82.6 2.5 %collective-permute-done.9 = f32[1,4096]{1,0:T(1,128)S(1)} collective-permute-done((f32[1,4096]{1,0:T(1,128)}, f32[1,4096]{1,0:T(1,128)S(1)}, u32[]{:S(2)}, u32[]{:S(2)}) %collective-permute-start.9) | collective-permute-done | bytes 16416 | tf_op jit(solution)/shard_map/ppermute | solution.py:285
  85.1 0.7 add_bitcast_fusion
  85.8 0.8 pad_maximum_fusion.6
  86.6 1.5 collective-permute-start.10
  88.1 3.6 %collective-permute-done.10 = f32[1,1,12288]{2,1,0:T(1,128)S(1)} collective-permute-done((f32[1,1,12288]{2,1,0:T(1,128)S(1)}, f32[1,1,12288]{2,1,0:T(1,128)S(1)}, u32[]{:S(2)}, u32[]{:S(2)}) %collective-permute-start.10) | collective-permute-done | bytes 49184 | tf_op jit(solution)/shard_map/ppermute | solution.py:285
  91.8 1.6 collective-permute-start.11
  93.4 3.1 %collective-permute-done.11 = f32[2,1,12288]{2,1,0:T(1,128)S(1)} collective-permute-done((f32[2,1,12288]{2,1,0:T(1,128)S(1)}, f32[2,1,12288]{2,1,0:T(1,128)S(1)}, u32[]{:S(2)}, u32[]{:S(2)}) %collective-permute-start.11) | collective-permute-done | bytes 98336 | tf_op jit(solution)/shard_map/ppermute | solution.py:285
  96.6 0.6 collective-permute-start.12
  97.2 5.1 %collective-permute-done.12 = f32[4,1,12288]{2,1,0:T(1,128)S(1)} collective-permute-done((f32[4,1,12288]{2,1,0:T(1,128)S(1)}, f32[4,1,12288]{2,1,0:T(1,128)S(1)}, u32[]{:S(2)}, u32[]{:S(2)}) %collective-permute-start.12) | collective-permute-done | bytes 196640 | tf_op jit(solution)/shard_map/ppermute | solution.py:285
  102.9 1.7 %collective-permute-done.13 = f32[8,1,12288]{2,1,0:T(1,128)S(1)} collective-permute-done((f32[8,1,12288]{2,1,0:T(1,128)S(1)}, f32[8,1,12288]{2,1,0:T(1,128)S(1)}, u32[]{:S(2)}, u32[]{:S(2)}) %collective-permute-start.13) | collective-permute-done | bytes 393248 | tf_op jit(solution)/shard_map/ppermute | solution.py:285
  104.8 0.7 broadcast_multiply_fusion
  105.5 26.7 %grad_rows.1 = f32[256,256]{1,0:T(8,128)} custom-call(s32[1]{0:T(128)} %bitcast.me_ref, bf16[256,256]{1,0:T(8,128)(2,1)} %refs_0_.1, bf16[65536,256]{1,0:T(8,128)(2,1)} %codes_ref.9, f32[1,256]{1,0:T(1,128)} %copy-done.9, f32[1,4096]{1,0:T(1,128)} %bitcast.5, f32[16,1,12288]{2,1,0:T(1,128)} %copy-done.3, f32[16,1,12288]{2,1,0:T(1,128)} %copy-done.3), custom_call_target="tpu_custom_call" | custom-call | tf_op jit(solution)/shard_map/grad_rows/pallas_call | solution.py:209
  132.2 1.5 collective-permute-start.14
  133.7 28.6 %grad_codes.1 = f32[4096,256]{1,0:T(8,128)} custom-call(s32[1]{0:T(128)} %bitcast.me_ref, bf16[65536,256]{1,0:T(8,128)(2,1)} %codes_ref.9, f32[16,1,256]{2,1,0:T(1,128)} %copy-done.8, f32[1,4096]{1,0:T(1,128)} %bitcast.6, f32[1,1,4096]{2,1,0:T(1,128)} %get-tuple-element.33.log_ref, f32[1,1,4096]{2,1,0:T(1,128)} %get-tuple-element.34.squares_ref, ...), custom_call_target="tpu_custom_call" | custom-call | tf_op jit(solution)/shard_map/grad_codes/pallas_call | solution.py:263
  162.3 0.7 add.16
  (46 shorter events, 2.3 us)
Async XLA Ops:
  0.6 18.3 %copy-start = (bf16[256,256]{1,0:T(8,128)(2,1)S(1)}, bf16[256,256]{1,0:T(8,128)(2,1)}, u32[]{:S(2)}) copy-start(bf16[256,256]{1,0:T(8,128)(2,1)} %refs_0_.1) | copy-start | bytes 393220
  0.6 18.3 %collective-permute-start = (bf16[256,256]{1,0:T(8,128)(2,1)}, bf16[256,256]{1,0:T(8,128)(2,1)S(1)}, u32[]{:S(2)}, u32[]{:S(2)}) collective-permute-start(bf16[256,256]{1,0:T(8,128)(2,1)} %refs_0_.1), channel_id=1, source_target_pairs={{0,16},{2,18},{4,20},{6,22},{8,24},{10,26},{12,28},{14,30},{16,0},... | collective-permute-start | bytes 393224 | tf_op jit(solution)/shard_map/ppermute | solution.py:285
  18.9 30.2 %copy-start.6 = (bf16[256,256]{1,0:T(8,128)(2,1)}, bf16[256,256]{1,0:T(8,128)(2,1)S(1)}, u32[]{:S(2)}) copy-start(bf16[256,256]{1,0:T(8,128)(2,1)S(1)} %collective-permute-done.refs_1_) | copy-start | bytes 393220
  19.0 15.8 %copy-start.1 = (bf16[256,256]{1,0:T(8,128)(2,1)S(1)}, bf16[256,256]{1,0:T(8,128)(2,1)}, u32[]{:S(2)}) copy-start(bf16[256,256]{1,0:T(8,128)(2,1)} %refs_0_.1) | copy-start | bytes 393220
  19.0 15.8 %collective-permute-start.1 = (bf16[512,256]{1,0:T(8,128)(2,1)S(1)}, bf16[512,256]{1,0:T(8,128)(2,1)S(1)}, u32[]{:S(2)}, u32[]{:S(2)}) collective-permute-start(bf16[512,256]{1,0:T(8,128)(2,1)S(1)} %pad_maximum_fusion.3), channel_id=1, source_target_pairs={{0,8},{2,10},{4,12},{6,14},{8,0},{10,2},{12,4},{14,6},{16,24},{18,... | collective-permute-start | bytes 786440 | tf_op jit(solution)/shard_map/ppermute | solution.py:285
  34.8 19.5 %copy-start.4 = (bf16[512,256]{1,0:T(8,128)(2,1)}, bf16[512,256]{1,0:T(8,128)(2,1)S(1)}, u32[]{:S(2)}) copy-start(bf16[512,256]{1,0:T(8,128)(2,1)S(1)} %collective-permute-done.1.refs_2_) | copy-start | bytes 786436
  34.8 14.3 %collective-permute-start.3 = (bf16[1024,256]{1,0:T(8,128)(2,1)S(1)}, bf16[1024,256]{1,0:T(8,128)(2,1)S(1)}, u32[]{:S(2)}, u32[]{:S(2)}) collective-permute-start(bf16[1024,256]{1,0:T(8,128)(2,1)S(1)} %pad_maximum_fusion.1), channel_id=1, source_target_pairs={{0,4},{2,6},{4,0},{6,2},{8,12},{10,14},{12,8},{14,10},{16,20},{18,... | collective-permute-start | bytes 1572872 | tf_op jit(solution)/shard_map/ppermute | solution.py:285
  36.4 3.8 %collective-permute-start.2 = (f32[2,256]{1,0:T(2,128)}, f32[2,256]{1,0:T(2,128)S(1)}, u32[]{:S(2)}, u32[]{:S(2)}) collective-permute-start(f32[2,256]{1,0:T(2,128)} %row_stats.3), channel_id=1, source_target_pairs={{0,1},{1,0},{2,3},{3,2},{4,5},{5,4},{6,7},{7,6},{8,9},{9,8},{10,11... | collective-permute-start | bytes 6152 | tf_op jit(solution)/shard_map/ppermute | solution.py:285
  41.0 40.1 %copy-start.9 = (f32[1,256]{1,0:T(1,128)}, f32[1,256]{1,0:T(1,128)S(1)}, u32[]{:S(2)}) copy-start(f32[1,256]{1,0:T(1,128)S(1)} %add_add_fusion.lse_ref) | copy-start | bytes 3076
  41.0 4.5 %collective-permute-start.4 = (f32[1,1,256]{2,1,0:T(1,128)S(1)}, f32[1,1,256]{2,1,0:T(1,128)S(1)}, u32[]{:S(2)}, u32[]{:S(2)}) collective-permute-start(f32[1,1,256]{2,1,0:T(1,128)S(1)} %bitcast.7), channel_id=1, source_target_pairs={{0,16},{2,18},{4,20},{6,22},{8,24},{10,26},{12,28},{14,30},{16,0},... | collective-permute-start | bytes 3080 | tf_op jit(solution)/shard_map/ppermute | solution.py:285
  45.5 3.6 %collective-permute-start.5 = (f32[2,1,256]{2,1,0:T(1,128)S(1)}, f32[2,1,256]{2,1,0:T(1,128)S(1)}, u32[]{:S(2)}, u32[]{:S(2)}) collective-permute-start(f32[2,1,256]{2,1,0:T(1,128)S(1)} %pad_maximum_fusion.9), channel_id=1, source_target_pairs={{0,8},{2,10},{4,12},{6,14},{8,0},{10,2},{12,4},{14,6},{16,24},{18,... | collective-permute-start | bytes 6152 | tf_op jit(solution)/shard_map/ppermute | solution.py:285
  49.1 5.1 %copy-start.2 = (bf16[1024,256]{1,0:T(8,128)(2,1)}, bf16[1024,256]{1,0:T(8,128)(2,1)S(1)}, u32[]{:S(2)}) copy-start(bf16[1024,256]{1,0:T(8,128)(2,1)S(1)} %collective-permute-done.3.refs_3_) | copy-start | bytes 1572868
  49.2 5.0 %collective-permute-start.8 = (bf16[2048,256]{1,0:T(8,128)(2,1)S(1)}, bf16[2048,256]{1,0:T(8,128)(2,1)S(1)}, u32[]{:S(2)}, u32[]{:S(2)}) collective-permute-start(bf16[2048,256]{1,0:T(8,128)(2,1)S(1)} %pad_maximum_fusion), channel_id=1, source_target_pairs={{0,2},{2,0},{4,6},{6,4},{8,10},{10,8},{12,14},{14,12},{16,18},{18,... | collective-permute-start | bytes 3145736 | tf_op jit(solution)/shard_map/ppermute | solution.py:285
  49.3 3.7 %collective-permute-start.6 = (f32[4,1,256]{2,1,0:T(1,128)S(1)}, f32[4,1,256]{2,1,0:T(1,128)S(1)}, u32[]{:S(2)}, u32[]{:S(2)}) collective-permute-start(f32[4,1,256]{2,1,0:T(1,128)S(1)} %pad_maximum_fusion.8), channel_id=1, source_target_pairs={{0,4},{2,6},{4,0},{6,2},{8,12},{10,14},{12,8},{14,10},{16,20},{18,... | collective-permute-start | bytes 12296 | tf_op jit(solution)/shard_map/ppermute | solution.py:285
  53.0 1.2 collective-permute-start.7
  54.3 0.6 copy-start.8
  54.3 1.0 copy-start.5
  81.1 4.0 %collective-permute-start.9 = (f32[1,4096]{1,0:T(1,128)}, f32[1,4096]{1,0:T(1,128)S(1)}, u32[]{:S(2)}, u32[]{:S(2)}) collective-permute-start(f32[1,4096]{1,0:T(1,128)} %get-tuple-element.35), channel_id=1, source_target_pairs={{0,1},{1,0},{2,3},{3,2},{4,5},{5,4},{6,7},{7,6},{8,9},{9,8},{10,11... | collective-permute-start | bytes 49160 | tf_op jit(solution)/shard_map/ppermute | solution.py:285
  86.6 5.1 %collective-permute-start.10 = (f32[1,1,12288]{2,1,0:T(1,128)S(1)}, f32[1,1,12288]{2,1,0:T(1,128)S(1)}, u32[]{:S(2)}, u32[]{:S(2)}) collective-permute-start(f32[1,1,12288]{2,1,0:T(1,128)S(1)} %pad_maximum_fusion.6), channel_id=1, source_target_pairs={{0,16},{2,18},{4,20},{6,22},{8,24},{10,26},{12,28},{14,30},{16,0},... | collective-permute-start | bytes 147464 | tf_op jit(solution)/shard_map/ppermute | solution.py:285
  91.8 4.7 %collective-permute-start.11 = (f32[2,1,12288]{2,1,0:T(1,128)S(1)}, f32[2,1,12288]{2,1,0:T(1,128)S(1)}, u32[]{:S(2)}, u32[]{:S(2)}) collective-permute-start(f32[2,1,12288]{2,1,0:T(1,128)S(1)} %pad_maximum_fusion.5), channel_id=1, source_target_pairs={{0,8},{2,10},{4,12},{6,14},{8,0},{10,2},{12,4},{14,6},{16,24},{18,... | collective-permute-start | bytes 294920 | tf_op jit(solution)/shard_map/ppermute | solution.py:285
  96.6 5.7 %collective-permute-start.12 = (f32[4,1,12288]{2,1,0:T(1,128)S(1)}, f32[4,1,12288]{2,1,0:T(1,128)S(1)}, u32[]{:S(2)}, u32[]{:S(2)}) collective-permute-start(f32[4,1,12288]{2,1,0:T(1,128)S(1)} %pad_maximum_fusion.4), channel_id=1, source_target_pairs={{0,4},{2,6},{4,0},{6,2},{8,12},{10,14},{12,8},{14,10},{16,20},{18,... | collective-permute-start | bytes 589832 | tf_op jit(solution)/shard_map/ppermute | solution.py:285
  102.8 1.8 %collective-permute-start.13 = (f32[8,1,12288]{2,1,0:T(1,128)S(1)}, f32[8,1,12288]{2,1,0:T(1,128)S(1)}, u32[]{:S(2)}, u32[]{:S(2)}) collective-permute-start(f32[8,1,12288]{2,1,0:T(1,128)S(1)} %pad_maximum_fusion.2), channel_id=1, source_target_pairs={{0,2},{2,0},{4,6},{6,4},{8,10},{10,8},{12,14},{14,12},{16,18},{18,... | collective-permute-start | bytes 1179656 | tf_op jit(solution)/shard_map/ppermute | solution.py:285
  104.6 0.9 copy-start.3
  132.2 30.1 %copy-start.7 = (f32[256,256]{1,0:T(8,128)S(1)}, f32[256,256]{1,0:T(8,128)}, u32[]{:S(2)}) copy-start(f32[256,256]{1,0:T(8,128)} %grad_rows.1) | copy-start | bytes 786436
  132.2 30.1 %collective-permute-start.14 = (f32[256,256]{1,0:T(8,128)}, f32[256,256]{1,0:T(8,128)S(1)}, u32[]{:S(2)}, u32[]{:S(2)}) collective-permute-start(f32[256,256]{1,0:T(8,128)} %grad_rows.1), channel_id=1, source_target_pairs={{0,1},{1,0},{2,3},{3,2},{4,5},{5,4},{6,7},{7,6},{8,9},{9,8},{10,11... | collective-permute-start | bytes 786440 | tf_op jit(solution)/shard_map/ppermute | solution.py:285

commit v3 on v2

--- a/solution.py
+++ b/solution.py
@@ -170,12 +170,14 @@
 def rows_call(me, encoded, codebook, row_lse, shift, gathered, devices, own):
     rows, features = encoded.shape
     codes = codebook.shape[0]
-    block = math.gcd(own, 4096)
-    per_device = own // block
-    chunk = math.gcd(block, 512)
-
-    def kernel(me_ref, encoded_ref, codes_ref, lse_ref, shift_ref, log_ref, squares_ref, out_ref, lse_wide, shift_wide):
-        @pl.when(pl.program_id(0) == 0)
+    span = math.gcd(devices, max(1, 8192 // own))
+    block = span * own
+    chunk = math.gcd(own, 512)
+
+    def kernel(me_ref, encoded_ref, codes_ref, lse_ref, shift_ref, vectors_ref, out_ref, lse_wide, shift_wide):
+        step = pl.program_id(0)
+
+        @pl.when(step == 0)
         def _():
             out_ref[...] = jnp.zeros(out_ref.shape, jnp.float32)
             mine = pl.ds(pl.multiple_of(me_ref[0] * rows, rows), rows)
@@ -185,11 +187,12 @@
         encoded_here = encoded_ref[...]
         total = out_ref[...]
         for k in range(block // chunk):
-            part = slice(k * chunk, (k + 1) * chunk)
-            code_rows = codes_ref[part, :]
+            code_rows = codes_ref[k * chunk : (k + 1) * chunk, :]
             scores = lax.dot_general(encoded_here, code_rows, NT, preferred_element_type=jnp.float32)
-            log_mass = log_ref[0, :, part]
-            squares = squares_ref[0, :, part]
+            owner, start = divmod(k * chunk, own)
+            place = place_of(me_ref[0] ^ (step * span + owner), devices)
+            log_mass = vectors_ref[place, :, start : start + chunk]
+            squares = vectors_ref[place, :, own + start : own + start + chunk]
             tiles = []
             for q in range(chunk // LANES):
                 lane = slice(q * LANES, (q + 1) * LANES)
@@ -199,12 +202,6 @@
             grad_tile = jnp.concatenate(tiles, axis=1)
             total = total + jnp.dot(grad_tile, code_rows, preferred_element_type=jnp.float32)
         out_ref[...] = total
-
-    def log_map(i, me):
-        return (place_of(me[0] ^ (i // per_device), devices), 0, i % per_device)
-
-    def squares_map(i, me):
-        return (place_of(me[0] ^ (i // per_device), devices), 0, per_device + i % per_device)
 
     return pl.pallas_call(
         kernel,
@@ -216,8 +213,7 @@
                 pl.BlockSpec((block, features), lambda i, me: (i, 0)),
                 pl.BlockSpec(row_lse.shape, lambda i, me: (0, 0)),
                 pl.BlockSpec(shift.shape, lambda i, me: (0, 0)),
-                pl.BlockSpec((1, 1, block), log_map),
-                pl.BlockSpec((1, 1, block), squares_map),
+                pl.BlockSpec((devices, 1, 2 * own), lambda i, me: (0, 0, 0)),
             ],
             out_specs=pl.BlockSpec((rows, features), lambda i, me: (0, 0)),
             scratch_shapes=[pltpu.VMEM((rows, LANES), jnp.float32)] * 2,
@@ -225,12 +221,12 @@
         out_shape=jax.ShapeDtypeStruct((rows, features), jnp.float32),
         compiler_params=PARAMS,
         name="grad_rows",
-    )(me, encoded, codebook, row_lse, shift, gathered, gathered)
-
-
-def codes_call(me, pieces, codebook, all_lse, shift, log_mass, squares, devices, own, CHAINS=1, BLOCK=512):
+    )(me, encoded, codebook, row_lse, shift, gathered)
+
+
+def codes_call(me, pieces, codebook, all_lse, shift, log_mass, squares, devices, own):
     rows, features = pieces[0].shape
-    block = math.gcd(own, BLOCK)
+    block = math.gcd(own, 1024)
     blocks = own // block
 
     def kernel(me_ref, codes_ref, lse_ref, shift_ref, log_ref, squares_ref, *refs):
@@ -238,7 +234,7 @@
         log_mass = row_to_columns(log_ref[0])
         half = row_to_columns(squares_ref[0])
         code_rows = codes_ref[...]
-        totals = [jnp.zeros((block, features), jnp.float32)] * CHAINS
+        total = jnp.zeros((block, features), jnp.float32)
         sums = jnp.zeros((block, LANES), jnp.float32)
         for p in range(devices):
             piece, start = piece_of(p, rows)
@@ -254,11 +250,9 @@
                 sums = sums + tile
                 tiles.append(tile.astype(jnp.bfloat16))
             grad_tile = jnp.concatenate(tiles, axis=1)
-            totals[p % CHAINS] = totals[p % CHAINS] + jnp.dot(
-                grad_tile, row_block, preferred_element_type=jnp.float32
-            )
+            total = total + jnp.dot(grad_tile, row_block, preferred_element_type=jnp.float32)
         code_sums = jnp.sum(sums, axis=1, keepdims=True)
-        out_ref[...] = sum(totals) - code_sums * code_rows.astype(jnp.float32)
+        out_ref[...] = total - code_sums * code_rows.astype(jnp.float32)
 
     return pl.pallas_call(
         kernel,
@@ -341,8 +335,13 @@
             all_lse = gather_more(all_lse)
 
     log_mass, squares, cross = mass_call(me, pieces, codebook, all_lse, devices, own)
-    cross = xor_sum(cross, "code")
+    offset = lax.axis_size("code") // 2
+    while offset > 1:
+        cross = cross + from_xor(cross, "code", offset)
+        offset //= 2
     message = jnp.concatenate([log_mass, squares, cross[None]], axis=2)
+    if offset:
+        message = message + jnp.pad(from_xor(cross, "code", offset)[None], ((0, 0), (0, 0), (2 * own, 0)))
     gathered = xor_gather(lax.optimization_barrier(message), "dp")
     shift = jnp.sum(gathered[:, :, 2 * own :], axis=0) * (-1.0 / LN2)
 

time: 164 us -> 159 us (0.970)
  Pallas kernels: 109 us -> 105 us
    pallas_call x1, Pallas kernels: 26.7 us -> 23.4 us  [rows_call(): pl.pallas_call(kernel, grid_spec=pltpu.PrefetchScalarGridSpec(num_scalar_...]
  transfers between devices with their start and end apart: 15 -> 15, of which waited for: 10 -> 10; matrix products, arithmetic and copies ran while one was open for 1% -> 1% of each run, Pallas kernels for 35% -> 36%
where the time goes in v3:
time: 159 us; the launch traced here: 158 us
  Pallas kernels  105 us (66%)
  waiting for transfers between devices  27.7 us (17%)
  starting transfers between devices  19.2 us (12%)
  other arithmetic  3.97 us (2%)
    pallas_call x2, Pallas kernels, stats_call(): pl.pallas_call(kernel, grid=((last - first) // block,), in_specs=[pl.Bloc...  28.3 us
    pallas_call x1, Pallas kernels, codes_call(): pl.pallas_call(kernel, grid_spec=pltpu.PrefetchScalarGridSpec(num_scalar_...  27.8 us
    ppermute x15, waiting for transfers between devices, from_xor(): lax.ppermute(values, axis, [(i, i ^ offset) for i in range(lax.axis_size(...  27.7 us
    pallas_call x1, Pallas kernels, mass_call(): pl.pallas_call(kernel, grid_spec=pltpu.PrefetchScalarGridSpec(num_scalar_...  25.8 us
    pallas_call x1, Pallas kernels, rows_call(): pl.pallas_call(kernel, grid_spec=pltpu.PrefetchScalarGridSpec(num_scalar_...  23.4 us
    ppermute x15, starting transfers between devices, from_xor(): lax.ppermute(values, axis, [(i, i ^ offset) for i in range(lax.axis_size(...  19.2 us
  transfers between devices with their start and end apart: 15, of which 10 were waited for; matrix products, arithmetic and copies ran while one was open for 1% of the time, Pallas kernels for 36%

profile of v3, /device:TPU:0, one launch (start us, length us, event | category | flops | bytes accessed | tf_op | source)
XLA Modules:
  0.0 158.2 jit_solution(7678892566662782264)
XLA Ops:
  0.6 4.1 %collective-permute-start = (bf16[256,256]{1,0:T(8,128)(2,1)}, bf16[256,256]{1,0:T(8,128)(2,1)S(1)}, u32[]{:S(2)}, u32[]{:S(2)}) collective-permute-start(bf16[256,256]{1,0:T(8,128)(2,1)} %refs_0_.1), channel_id=1, source_target_pairs={{0,16},{2,18},{4,20},{6,22},{8,24},{10,26},{12,28},{14,30},{16,0},... | collective-permute-start | bytes 393224 | tf_op jit(solution)/shard_map/ppermute | solution.py:279
  4.7 14.2 %row_stats.2.state_ref = f32[2,8,256]{2,1,0:T(8,128)} custom-call(bf16[256,256]{1,0:T(8,128)(2,1)} %refs_0_.1, bf16[65536,256]{1,0:T(8,128)(2,1)} %codes_ref.9, f32[2,8,256]{2,1,0:T(8,128)} %constant.5.clone.1.state_ref), custom_call_target="tpu_custom_call" | custom-call | tf_op jit(solution)/shard_map/row_stats/pallas_call | solution.py:70
  19.0 1.6 %collective-permute-start.1 = (bf16[512,256]{1,0:T(8,128)(2,1)S(1)}, bf16[512,256]{1,0:T(8,128)(2,1)S(1)}, u32[]{:S(2)}, u32[]{:S(2)}) collective-permute-start(bf16[512,256]{1,0:T(8,128)(2,1)S(1)} %pad_maximum_fusion.3), channel_id=1, source_target_pairs={{0,8},{2,10},{4,12},{6,14},{8,0},{10,2},{12,4},{14,6},{16,24},{18,... | collective-permute-start | bytes 786440 | tf_op jit(solution)/shard_map/ppermute | solution.py:279
  20.6 14.2 %row_stats.3 = f32[2,256]{1,0:T(2,128)} custom-call(bf16[256,256]{1,0:T(8,128)(2,1)} %refs_0_.1, bf16[65536,256]{1,0:T(8,128)(2,1)} %codes_ref.9, f32[2,8,256]{2,1,0:T(8,128)} %row_stats.2.state_ref), custom_call_target="tpu_custom_call" | custom-call | tf_op jit(solution)/shard_map/row_stats/pallas_call | solution.py:70
  34.8 1.6 %collective-permute-start.3 = (bf16[1024,256]{1,0:T(8,128)(2,1)S(1)}, bf16[1024,256]{1,0:T(8,128)(2,1)S(1)}, u32[]{:S(2)}, u32[]{:S(2)}) collective-permute-start(bf16[1024,256]{1,0:T(8,128)(2,1)S(1)} %pad_maximum_fusion.1), channel_id=1, source_target_pairs={{0,4},{2,6},{4,0},{6,2},{8,12},{10,14},{12,8},{14,10},{16,20},{18,... | collective-permute-start | bytes 1572872 | tf_op jit(solution)/shard_map/ppermute | solution.py:279
  36.4 1.5 collective-permute-start.2
  37.9 2.3 %collective-permute-done.2 = f32[2,256]{1,0:T(2,128)S(1)} collective-permute-done((f32[2,256]{1,0:T(2,128)}, f32[2,256]{1,0:T(2,128)S(1)}, u32[]{:S(2)}, u32[]{:S(2)}) %collective-permute-start.2) | collective-permute-done | bytes 2080 | tf_op jit(solution)/shard_map/ppermute | solution.py:279
  40.2 0.8 add_add_fusion.lse_ref
  41.0 1.5 collective-permute-start.4
  42.5 3.1 %collective-permute-done.4 = f32[1,1,256]{2,1,0:T(1,128)S(1)} collective-permute-done((f32[1,1,256]{2,1,0:T(1,128)S(1)}, f32[1,1,256]{2,1,0:T(1,128)S(1)}, u32[]{:S(2)}, u32[]{:S(2)}) %collective-permute-start.4) | collective-permute-done | bytes 1056 | tf_op jit(solution)/shard_map/ppermute | solution.py:279
  45.5 1.5 collective-permute-start.5
  47.0 2.1 %collective-permute-done.5 = f32[2,1,256]{2,1,0:T(1,128)S(1)} collective-permute-done((f32[2,1,256]{2,1,0:T(1,128)S(1)}, f32[2,1,256]{2,1,0:T(1,128)S(1)}, u32[]{:S(2)}, u32[]{:S(2)}) %collective-permute-start.5) | collective-permute-done | bytes 2080 | tf_op jit(solution)/shard_map/ppermute | solution.py:279
  49.3 0.6 collective-permute-start.6
  49.9 3.1 %collective-permute-done.6 = f32[4,1,256]{2,1,0:T(1,128)S(1)} collective-permute-done((f32[4,1,256]{2,1,0:T(1,128)S(1)}, f32[4,1,256]{2,1,0:T(1,128)S(1)}, u32[]{:S(2)}, u32[]{:S(2)}) %collective-permute-start.6) | collective-permute-done | bytes 4128 | tf_op jit(solution)/shard_map/ppermute | solution.py:279
  53.1 1.1 collective-permute-done.7
  54.3 0.6 copy-done.8
  55.3 25.8 %code_mass.1 = (f32[1,1,4096]{2,1,0:T(1,128)}, f32[1,1,4096]{2,1,0:T(1,128)}, f32[1,4096]{1,0:T(1,128)}) custom-call(s32[1]{0:T(128)} %bitcast.me_ref, bf16[65536,256]{1,0:T(8,128)(2,1)} %codes_ref.9, f32[16,1,256]{2,1,0:T(1,128)} %copy-done.8, bf16[256,256]{1,0:T(8,128)(2,1)} %refs_0_.1, bf16[256,256]{1,0:T(8,128)(2,1)} %copy-done.5, ...), custom_call_target="tpu_custom_call" | custom-call | tf_op jit(solution)/shard_map/code_mass/pallas_call | solution.py:140
  81.1 1.6 collective-permute-start.9
  82.6 2.5 %collective-permute-done.9 = f32[1,4096]{1,0:T(1,128)S(1)} collective-permute-done((f32[1,4096]{1,0:T(1,128)}, f32[1,4096]{1,0:T(1,128)S(1)}, u32[]{:S(2)}, u32[]{:S(2)}) %collective-permute-start.9) | collective-permute-done | bytes 16416 | tf_op jit(solution)/shard_map/ppermute | solution.py:279
  85.1 0.8 maximum_add_fusion
  85.9 1.5 collective-permute-start.10
  87.4 3.6 %collective-permute-done.10 = f32[1,1,12288]{2,1,0:T(1,128)S(1)} collective-permute-done((f32[1,1,12288]{2,1,0:T(1,128)S(1)}, f32[1,1,12288]{2,1,0:T(1,128)S(1)}, u32[]{:S(2)}, u32[]{:S(2)}) %collective-permute-start.10) | collective-permute-done | bytes 49184 | tf_op jit(solution)/shard_map/ppermute | solution.py:279
  91.1 1.6 collective-permute-start.11
  92.6 3.1 %collective-permute-done.11 = f32[2,1,12288]{2,1,0:T(1,128)S(1)} collective-permute-done((f32[2,1,12288]{2,1,0:T(1,128)S(1)}, f32[2,1,12288]{2,1,0:T(1,128)S(1)}, u32[]{:S(2)}, u32[]{:S(2)}) %collective-permute-start.11) | collective-permute-done | bytes 98336 | tf_op jit(solution)/shard_map/ppermute | solution.py:279
  95.9 0.6 collective-permute-start.12
  96.5 5.1 %collective-permute-done.12 = f32[4,1,12288]{2,1,0:T(1,128)S(1)} collective-permute-done((f32[4,1,12288]{2,1,0:T(1,128)S(1)}, f32[4,1,12288]{2,1,0:T(1,128)S(1)}, u32[]{:S(2)}, u32[]{:S(2)}) %collective-permute-start.12) | collective-permute-done | bytes 196640 | tf_op jit(solution)/shard_map/ppermute | solution.py:279
  102.2 1.7 %collective-permute-done.13 = f32[8,1,12288]{2,1,0:T(1,128)S(1)} collective-permute-done((f32[8,1,12288]{2,1,0:T(1,128)S(1)}, f32[8,1,12288]{2,1,0:T(1,128)S(1)}, u32[]{:S(2)}, u32[]{:S(2)}) %collective-permute-start.13) | collective-permute-done | bytes 393248 | tf_op jit(solution)/shard_map/ppermute | solution.py:279
  104.1 0.7 broadcast_multiply_fusion
  104.8 23.4 %grad_rows.1 = f32[256,256]{1,0:T(8,128)} custom-call(s32[1]{0:T(128)} %bitcast.me_ref, bf16[256,256]{1,0:T(8,128)(2,1)} %refs_0_.1, bf16[65536,256]{1,0:T(8,128)(2,1)} %codes_ref.9, f32[1,256]{1,0:T(1,128)} %copy-done.9, f32[1,4096]{1,0:T(1,128)} %bitcast.5, f32[16,1,12288]{2,1,0:T(1,128)} %copy-done.6), custom_call_target="tpu_custom_call" | custom-call | tf_op jit(solution)/shard_map/grad_rows/pallas_call | solution.py:206
  128.1 1.5 collective-permute-start.14
  129.6 27.8 %grad_codes.1 = f32[4096,256]{1,0:T(8,128)} custom-call(s32[1]{0:T(128)} %bitcast.me_ref, bf16[65536,256]{1,0:T(8,128)(2,1)} %codes_ref.9, f32[16,1,256]{2,1,0:T(1,128)} %copy-done.8, f32[1,4096]{1,0:T(1,128)} %bitcast.6, f32[1,1,4096]{2,1,0:T(1,128)} %get-tuple-element.33.log_ref, f32[1,1,4096]{2,1,0:T(1,128)} %get-tuple-element.34.squares_ref, ...), custom_call_target="tpu_custom_call" | custom-call | tf_op jit(solution)/shard_map/grad_codes/pallas_call | solution.py:257
  157.5 0.7 add.18
  (45 shorter events, 1.7 us)
Async XLA Ops:
  0.6 18.3 %copy-start = (bf16[256,256]{1,0:T(8,128)(2,1)S(1)}, bf16[256,256]{1,0:T(8,128)(2,1)}, u32[]{:S(2)}) copy-start(bf16[256,256]{1,0:T(8,128)(2,1)} %refs_0_.1) | copy-start | bytes 393220
  0.6 18.3 %collective-permute-start = (bf16[256,256]{1,0:T(8,128)(2,1)}, bf16[256,256]{1,0:T(8,128)(2,1)S(1)}, u32[]{:S(2)}, u32[]{:S(2)}) collective-permute-start(bf16[256,256]{1,0:T(8,128)(2,1)} %refs_0_.1), channel_id=1, source_target_pairs={{0,16},{2,18},{4,20},{6,22},{8,24},{10,26},{12,28},{14,30},{16,0},... | collective-permute-start | bytes 393224 | tf_op jit(solution)/shard_map/ppermute | solution.py:279
  18.9 30.2 %copy-start.5 = (bf16[256,256]{1,0:T(8,128)(2,1)}, bf16[256,256]{1,0:T(8,128)(2,1)S(1)}, u32[]{:S(2)}) copy-start(bf16[256,256]{1,0:T(8,128)(2,1)S(1)} %collective-permute-done.refs_1_) | copy-start | bytes 393220
  19.0 15.8 %copy-start.1 = (bf16[256,256]{1,0:T(8,128)(2,1)S(1)}, bf16[256,256]{1,0:T(8,128)(2,1)}, u32[]{:S(2)}) copy-start(bf16[256,256]{1,0:T(8,128)(2,1)} %refs_0_.1) | copy-start | bytes 393220
  19.0 15.8 %collective-permute-start.1 = (bf16[512,256]{1,0:T(8,128)(2,1)S(1)}, bf16[512,256]{1,0:T(8,128)(2,1)S(1)}, u32[]{:S(2)}, u32[]{:S(2)}) collective-permute-start(bf16[512,256]{1,0:T(8,128)(2,1)S(1)} %pad_maximum_fusion.3), channel_id=1, source_target_pairs={{0,8},{2,10},{4,12},{6,14},{8,0},{10,2},{12,4},{14,6},{16,24},{18,... | collective-permute-start | bytes 786440 | tf_op jit(solution)/shard_map/ppermute | solution.py:279
  34.8 19.5 %copy-start.3 = (bf16[512,256]{1,0:T(8,128)(2,1)}, bf16[512,256]{1,0:T(8,128)(2,1)S(1)}, u32[]{:S(2)}) copy-start(bf16[512,256]{1,0:T(8,128)(2,1)S(1)} %collective-permute-done.1.refs_2_) | copy-start | bytes 786436
  34.8 14.3 %collective-permute-start.3 = (bf16[1024,256]{1,0:T(8,128)(2,1)S(1)}, bf16[1024,256]{1,0:T(8,128)(2,1)S(1)}, u32[]{:S(2)}, u32[]{:S(2)}) collective-permute-start(bf16[1024,256]{1,0:T(8,128)(2,1)S(1)} %pad_maximum_fusion.1), channel_id=1, source_target_pairs={{0,4},{2,6},{4,0},{6,2},{8,12},{10,14},{12,8},{14,10},{16,20},{18,... | collective-permute-start | bytes 1572872 | tf_op jit(solution)/shard_map/ppermute | solution.py:279
  36.4 3.8 %collective-permute-start.2 = (f32[2,256]{1,0:T(2,128)}, f32[2,256]{1,0:T(2,128)S(1)}, u32[]{:S(2)}, u32[]{:S(2)}) collective-permute-start(f32[2,256]{1,0:T(2,128)} %row_stats.3), channel_id=1, source_target_pairs={{0,1},{1,0},{2,3},{3,2},{4,5},{5,4},{6,7},{7,6},{8,9},{9,8},{10,11... | collective-permute-start | bytes 6152 | tf_op jit(solution)/shard_map/ppermute | solution.py:279
  41.0 40.1 %copy-start.9 = (f32[1,256]{1,0:T(1,128)}, f32[1,256]{1,0:T(1,128)S(1)}, u32[]{:S(2)}) copy-start(f32[1,256]{1,0:T(1,128)S(1)} %add_add_fusion.lse_ref) | copy-start | bytes 3076
  41.0 4.5 %collective-permute-start.4 = (f32[1,1,256]{2,1,0:T(1,128)S(1)}, f32[1,1,256]{2,1,0:T(1,128)S(1)}, u32[]{:S(2)}, u32[]{:S(2)}) collective-permute-start(f32[1,1,256]{2,1,0:T(1,128)S(1)} %bitcast.7), channel_id=1, source_target_pairs={{0,16},{2,18},{4,20},{6,22},{8,24},{10,26},{12,28},{14,30},{16,0},... | collective-permute-start | bytes 3080 | tf_op jit(solution)/shard_map/ppermute | solution.py:279
  45.5 3.6 %collective-permute-start.5 = (f32[2,1,256]{2,1,0:T(1,128)S(1)}, f32[2,1,256]{2,1,0:T(1,128)S(1)}, u32[]{:S(2)}, u32[]{:S(2)}) collective-permute-start(f32[2,1,256]{2,1,0:T(1,128)S(1)} %pad_maximum_fusion.8), channel_id=1, source_target_pairs={{0,8},{2,10},{4,12},{6,14},{8,0},{10,2},{12,4},{14,6},{16,24},{18,... | collective-permute-start | bytes 6152 | tf_op jit(solution)/shard_map/ppermute | solution.py:279
  49.1 5.1 %copy-start.2 = (bf16[1024,256]{1,0:T(8,128)(2,1)}, bf16[1024,256]{1,0:T(8,128)(2,1)S(1)}, u32[]{:S(2)}) copy-start(bf16[1024,256]{1,0:T(8,128)(2,1)S(1)} %collective-permute-done.3.refs_3_) | copy-start | bytes 1572868
  49.2 5.0 %collective-permute-start.8 = (bf16[2048,256]{1,0:T(8,128)(2,1)S(1)}, bf16[2048,256]{1,0:T(8,128)(2,1)S(1)}, u32[]{:S(2)}, u32[]{:S(2)}) collective-permute-start(bf16[2048,256]{1,0:T(8,128)(2,1)S(1)} %pad_maximum_fusion), channel_id=1, source_target_pairs={{0,2},{2,0},{4,6},{6,4},{8,10},{10,8},{12,14},{14,12},{16,18},{18,... | collective-permute-start | bytes 3145736 | tf_op jit(solution)/shard_map/ppermute | solution.py:279
  49.3 3.7 %collective-permute-start.6 = (f32[4,1,256]{2,1,0:T(1,128)S(1)}, f32[4,1,256]{2,1,0:T(1,128)S(1)}, u32[]{:S(2)}, u32[]{:S(2)}) collective-permute-start(f32[4,1,256]{2,1,0:T(1,128)S(1)} %pad_maximum_fusion.7), channel_id=1, source_target_pairs={{0,4},{2,6},{4,0},{6,2},{8,12},{10,14},{12,8},{14,10},{16,20},{18,... | collective-permute-start | bytes 12296 | tf_op jit(solution)/shard_map/ppermute | solution.py:279
  53.0 1.2 collective-permute-start.7
  54.3 0.6 copy-start.8
  54.3 1.0 copy-start.4
  81.1 4.0 %collective-permute-start.9 = (f32[1,4096]{1,0:T(1,128)}, f32[1,4096]{1,0:T(1,128)S(1)}, u32[]{:S(2)}, u32[]{:S(2)}) collective-permute-start(f32[1,4096]{1,0:T(1,128)} %get-tuple-element.35), channel_id=1, source_target_pairs={{0,1},{1,0},{2,3},{3,2},{4,5},{5,4},{6,7},{7,6},{8,9},{9,8},{10,11... | collective-permute-start | bytes 49160 | tf_op jit(solution)/shard_map/ppermute | solution.py:279
  85.9 5.1 %collective-permute-start.10 = (f32[1,1,12288]{2,1,0:T(1,128)S(1)}, f32[1,1,12288]{2,1,0:T(1,128)S(1)}, u32[]{:S(2)}, u32[]{:S(2)}) collective-permute-start(f32[1,1,12288]{2,1,0:T(1,128)S(1)} %maximum_add_fusion), channel_id=1, source_target_pairs={{0,16},{2,18},{4,20},{6,22},{8,24},{10,26},{12,28},{14,30},{16,0},... | collective-permute-start | bytes 147464 | tf_op jit(solution)/shard_map/ppermute | solution.py:279
  91.1 4.7 %collective-permute-start.11 = (f32[2,1,12288]{2,1,0:T(1,128)S(1)}, f32[2,1,12288]{2,1,0:T(1,128)S(1)}, u32[]{:S(2)}, u32[]{:S(2)}) collective-permute-start(f32[2,1,12288]{2,1,0:T(1,128)S(1)} %pad_maximum_fusion.5), channel_id=1, source_target_pairs={{0,8},{2,10},{4,12},{6,14},{8,0},{10,2},{12,4},{14,6},{16,24},{18,... | collective-permute-start | bytes 294920 | tf_op jit(solution)/shard_map/ppermute | solution.py:279
  95.9 5.7 %collective-permute-start.12 = (f32[4,1,12288]{2,1,0:T(1,128)S(1)}, f32[4,1,12288]{2,1,0:T(1,128)S(1)}, u32[]{:S(2)}, u32[]{:S(2)}) collective-permute-start(f32[4,1,12288]{2,1,0:T(1,128)S(1)} %pad_maximum_fusion.4), channel_id=1, source_target_pairs={{0,4},{2,6},{4,0},{6,2},{8,12},{10,14},{12,8},{14,10},{16,20},{18,... | collective-permute-start | bytes 589832 | tf_op jit(solution)/shard_map/ppermute | solution.py:279
  102.1 1.8 %collective-permute-start.13 = (f32[8,1,12288]{2,1,0:T(1,128)S(1)}, f32[8,1,12288]{2,1,0:T(1,128)S(1)}, u32[]{:S(2)}, u32[]{:S(2)}) collective-permute-start(f32[8,1,12288]{2,1,0:T(1,128)S(1)} %pad_maximum_fusion.2), channel_id=1, source_target_pairs={{0,2},{2,0},{4,6},{6,4},{8,10},{10,8},{12,14},{14,12},{16,18},{18,... | collective-permute-start | bytes 1179656 | tf_op jit(solution)/shard_map/ppermute | solution.py:279
  103.9 0.9 copy-start.6
  128.1 29.3 %copy-start.7 = (f32[256,256]{1,0:T(8,128)S(1)}, f32[256,256]{1,0:T(8,128)}, u32[]{:S(2)}) copy-start(f32[256,256]{1,0:T(8,128)} %grad_rows.1) | copy-start | bytes 786436
  128.1 29.3 %collective-permute-start.14 = (f32[256,256]{1,0:T(8,128)}, f32[256,256]{1,0:T(8,128)S(1)}, u32[]{:S(2)}, u32[]{:S(2)}) collective-permute-start(f32[256,256]{1,0:T(8,128)} %grad_rows.1), channel_id=1, source_target_pairs={{0,1},{1,0},{2,3},{3,2},{4,5},{5,4},{6,7},{7,6},{8,9},{9,8},{10,11... | collective-permute-start | bytes 786440 | tf_op jit(solution)/shard_map/ppermute | solution.py:279

commit v4 on v3

--- a/solution.py
+++ b/solution.py
@@ -96,7 +96,7 @@
 def mass_call(me, pieces, codebook, all_lse, devices, own):
     rows, features = pieces[0].shape
     total_rows = rows * devices
-    block = math.gcd(own, 512)
+    block = math.gcd(own, 1024)
     steps = own // block
 
     def kernel(me_ref, codes_ref, lse_ref, *refs):

time: 159 us -> 158 us (level)
  no operation moved by 1% of the time
where the time goes in v4:
time: 158 us
  Pallas kernels  105 us (66%)
  waiting for transfers between devices  27.7 us (18%)
  starting transfers between devices  19.2 us (12%)
  other arithmetic  3.97 us (3%)
    pallas_call x2, Pallas kernels, stats_call(): pl.pallas_call(kernel, grid=((last - first) // block,), in_specs=[pl.Bloc...  28.3 us
    pallas_call x1, Pallas kernels, codes_call(): pl.pallas_call(kernel, grid_spec=pltpu.PrefetchScalarGridSpec(num_scalar_...  27.9 us
    ppermute x15, waiting for transfers between devices, from_xor(): lax.ppermute(values, axis, [(i, i ^ offset) for i in range(lax.axis_size(...  27.7 us
    pallas_call x1, Pallas kernels, mass_call(): pl.pallas_call(kernel, grid_spec=pltpu.PrefetchScalarGridSpec(num_scalar_...  25.1 us
    pallas_call x1, Pallas kernels, rows_call(): pl.pallas_call(kernel, grid_spec=pltpu.PrefetchScalarGridSpec(num_scalar_...  23.3 us
    ppermute x15, starting transfers between devices, from_xor(): lax.ppermute(values, axis, [(i, i ^ offset) for i in range(lax.axis_size(...  19.2 us
  transfers between devices with their start and end apart: 15, of which 10 were waited for; matrix products, arithmetic and copies ran while one was open for 1% of the time, Pallas kernels for 36%

profile of v4, /device:TPU:0, one launch (start us, length us, event | category | flops | bytes accessed | tf_op | source)
XLA Modules:
  0.0 157.5 jit_solution(9091560996497350160)
XLA Ops:
  0.6 4.1 %collective-permute-start = (bf16[256,256]{1,0:T(8,128)(2,1)}, bf16[256,256]{1,0:T(8,128)(2,1)S(1)}, u32[]{:S(2)}, u32[]{:S(2)}) collective-permute-start(bf16[256,256]{1,0:T(8,128)(2,1)} %refs_0_.1), channel_id=1, source_target_pairs={{0,16},{2,18},{4,20},{6,22},{8,24},{10,26},{12,28},{14,30},{16,0},... | collective-permute-start | bytes 393224 | tf_op jit(solution)/shard_map/ppermute | solution.py:279
  4.7 14.2 %row_stats.2.state_ref = f32[2,8,256]{2,1,0:T(8,128)} custom-call(bf16[256,256]{1,0:T(8,128)(2,1)} %refs_0_.1, bf16[65536,256]{1,0:T(8,128)(2,1)} %codes_ref.9, f32[2,8,256]{2,1,0:T(8,128)} %constant.5.clone.1.state_ref), custom_call_target="tpu_custom_call" | custom-call | tf_op jit(solution)/shard_map/row_stats/pallas_call | solution.py:70
  19.0 1.6 %collective-permute-start.1 = (bf16[512,256]{1,0:T(8,128)(2,1)S(1)}, bf16[512,256]{1,0:T(8,128)(2,1)S(1)}, u32[]{:S(2)}, u32[]{:S(2)}) collective-permute-start(bf16[512,256]{1,0:T(8,128)(2,1)S(1)} %pad_maximum_fusion.3), channel_id=1, source_target_pairs={{0,8},{2,10},{4,12},{6,14},{8,0},{10,2},{12,4},{14,6},{16,24},{18,... | collective-permute-start | bytes 786440 | tf_op jit(solution)/shard_map/ppermute | solution.py:279
  20.6 14.2 %row_stats.3 = f32[2,256]{1,0:T(2,128)} custom-call(bf16[256,256]{1,0:T(8,128)(2,1)} %refs_0_.1, bf16[65536,256]{1,0:T(8,128)(2,1)} %codes_ref.9, f32[2,8,256]{2,1,0:T(8,128)} %row_stats.2.state_ref), custom_call_target="tpu_custom_call" | custom-call | tf_op jit(solution)/shard_map/row_stats/pallas_call | solution.py:70
  34.8 1.6 %collective-permute-start.3 = (bf16[1024,256]{1,0:T(8,128)(2,1)S(1)}, bf16[1024,256]{1,0:T(8,128)(2,1)S(1)}, u32[]{:S(2)}, u32[]{:S(2)}) collective-permute-start(bf16[1024,256]{1,0:T(8,128)(2,1)S(1)} %pad_maximum_fusion.1), channel_id=1, source_target_pairs={{0,4},{2,6},{4,0},{6,2},{8,12},{10,14},{12,8},{14,10},{16,20},{18,... | collective-permute-start | bytes 1572872 | tf_op jit(solution)/shard_map/ppermute | solution.py:279
  36.4 1.5 collective-permute-start.2
  37.9 2.3 %collective-permute-done.2 = f32[2,256]{1,0:T(2,128)S(1)} collective-permute-done((f32[2,256]{1,0:T(2,128)}, f32[2,256]{1,0:T(2,128)S(1)}, u32[]{:S(2)}, u32[]{:S(2)}) %collective-permute-start.2) | collective-permute-done | bytes 2080 | tf_op jit(solution)/shard_map/ppermute | solution.py:279
  40.2 0.8 add_add_fusion.lse_ref
  41.0 1.5 collective-permute-start.4
  42.5 3.1 %collective-permute-done.4 = f32[1,1,256]{2,1,0:T(1,128)S(1)} collective-permute-done((f32[1,1,256]{2,1,0:T(1,128)S(1)}, f32[1,1,256]{2,1,0:T(1,128)S(1)}, u32[]{:S(2)}, u32[]{:S(2)}) %collective-permute-start.4) | collective-permute-done | bytes 1056 | tf_op jit(solution)/shard_map/ppermute | solution.py:279
  45.5 1.5 collective-permute-start.5
  47.0 2.1 %collective-permute-done.5 = f32[2,1,256]{2,1,0:T(1,128)S(1)} collective-permute-done((f32[2,1,256]{2,1,0:T(1,128)S(1)}, f32[2,1,256]{2,1,0:T(1,128)S(1)}, u32[]{:S(2)}, u32[]{:S(2)}) %collective-permute-start.5) | collective-permute-done | bytes 2080 | tf_op jit(solution)/shard_map/ppermute | solution.py:279
  49.3 0.6 collective-permute-start.6
  49.9 3.1 %collective-permute-done.6 = f32[4,1,256]{2,1,0:T(1,128)S(1)} collective-permute-done((f32[4,1,256]{2,1,0:T(1,128)S(1)}, f32[4,1,256]{2,1,0:T(1,128)S(1)}, u32[]{:S(2)}, u32[]{:S(2)}) %collective-permute-start.6) | collective-permute-done | bytes 4128 | tf_op jit(solution)/shard_map/ppermute | solution.py:279
  53.1 1.1 collective-permute-done.7
  54.3 0.6 copy-done.8
  55.3 25.1 %code_mass.1 = (f32[1,1,4096]{2,1,0:T(1,128)}, f32[1,1,4096]{2,1,0:T(1,128)}, f32[1,4096]{1,0:T(1,128)}) custom-call(s32[1]{0:T(128)} %bitcast.me_ref, bf16[65536,256]{1,0:T(8,128)(2,1)} %codes_ref.9, f32[16,1,256]{2,1,0:T(1,128)} %copy-done.8, bf16[256,256]{1,0:T(8,128)(2,1)} %refs_0_.1, bf16[256,256]{1,0:T(8,128)(2,1)} %copy-done.5, ...), custom_call_target="tpu_custom_call" | custom-call | tf_op jit(solution)/shard_map/code_mass/pallas_call | solution.py:140
  80.4 1.6 collective-permute-start.9
  81.9 2.5 %collective-permute-done.9 = f32[1,4096]{1,0:T(1,128)S(1)} collective-permute-done((f32[1,4096]{1,0:T(1,128)}, f32[1,4096]{1,0:T(1,128)S(1)}, u32[]{:S(2)}, u32[]{:S(2)}) %collective-permute-start.9) | collective-permute-done | bytes 16416 | tf_op jit(solution)/shard_map/ppermute | solution.py:279
  84.4 0.8 maximum_add_fusion
  85.2 1.5 collective-permute-start.10
  86.6 3.6 %collective-permute-done.10 = f32[1,1,12288]{2,1,0:T(1,128)S(1)} collective-permute-done((f32[1,1,12288]{2,1,0:T(1,128)S(1)}, f32[1,1,12288]{2,1,0:T(1,128)S(1)}, u32[]{:S(2)}, u32[]{:S(2)}) %collective-permute-start.10) | collective-permute-done | bytes 49184 | tf_op jit(solution)/shard_map/ppermute | solution.py:279
  90.3 1.6 %collective-permute-start.11 = (f32[2,1,12288]{2,1,0:T(1,128)S(1)}, f32[2,1,12288]{2,1,0:T(1,128)S(1)}, u32[]{:S(2)}, u32[]{:S(2)}) collective-permute-start(f32[2,1,12288]{2,1,0:T(1,128)S(1)} %pad_maximum_fusion.5), channel_id=1, source_target_pairs={{0,8},{2,10},{4,12},{6,14},{8,0},{10,2},{12,4},{14,6},{16,24},{18,... | collective-permute-start | bytes 294920 | tf_op jit(solution)/shard_map/ppermute | solution.py:279
  91.9 3.1 %collective-permute-done.11 = f32[2,1,12288]{2,1,0:T(1,128)S(1)} collective-permute-done((f32[2,1,12288]{2,1,0:T(1,128)S(1)}, f32[2,1,12288]{2,1,0:T(1,128)S(1)}, u32[]{:S(2)}, u32[]{:S(2)}) %collective-permute-start.11) | collective-permute-done | bytes 98336 | tf_op jit(solution)/shard_map/ppermute | solution.py:279
  95.2 0.6 collective-permute-start.12
  95.8 5.2 %collective-permute-done.12 = f32[4,1,12288]{2,1,0:T(1,128)S(1)} collective-permute-done((f32[4,1,12288]{2,1,0:T(1,128)S(1)}, f32[4,1,12288]{2,1,0:T(1,128)S(1)}, u32[]{:S(2)}, u32[]{:S(2)}) %collective-permute-start.12) | collective-permute-done | bytes 196640 | tf_op jit(solution)/shard_map/ppermute | solution.py:279
  101.5 1.7 %collective-permute-done.13 = f32[8,1,12288]{2,1,0:T(1,128)S(1)} collective-permute-done((f32[8,1,12288]{2,1,0:T(1,128)S(1)}, f32[8,1,12288]{2,1,0:T(1,128)S(1)}, u32[]{:S(2)}, u32[]{:S(2)}) %collective-permute-start.13) | collective-permute-done | bytes 393248 | tf_op jit(solution)/shard_map/ppermute | solution.py:279
  103.3 0.7 broadcast_multiply_fusion
  104.1 23.3 %grad_rows.1 = f32[256,256]{1,0:T(8,128)} custom-call(s32[1]{0:T(128)} %bitcast.me_ref, bf16[256,256]{1,0:T(8,128)(2,1)} %refs_0_.1, bf16[65536,256]{1,0:T(8,128)(2,1)} %codes_ref.9, f32[1,256]{1,0:T(1,128)} %copy-done.9, f32[1,4096]{1,0:T(1,128)} %bitcast.5, f32[16,1,12288]{2,1,0:T(1,128)} %copy-done.6), custom_call_target="tpu_custom_call" | custom-call | tf_op jit(solution)/shard_map/grad_rows/pallas_call | solution.py:206
  127.4 1.5 collective-permute-start.14
  128.9 27.9 %grad_codes.1 = f32[4096,256]{1,0:T(8,128)} custom-call(s32[1]{0:T(128)} %bitcast.me_ref, bf16[65536,256]{1,0:T(8,128)(2,1)} %codes_ref.9, f32[16,1,256]{2,1,0:T(1,128)} %copy-done.8, f32[1,4096]{1,0:T(1,128)} %bitcast.6, f32[1,1,4096]{2,1,0:T(1,128)} %get-tuple-element.33.log_ref, f32[1,1,4096]{2,1,0:T(1,128)} %get-tuple-element.34.squares_ref, ...), custom_call_target="tpu_custom_call" | custom-call | tf_op jit(solution)/shard_map/grad_codes/pallas_call | solution.py:257
  156.8 0.7 add.18
  (45 shorter events, 1.7 us)
Async XLA Ops:
  0.6 18.3 %copy-start = (bf16[256,256]{1,0:T(8,128)(2,1)S(1)}, bf16[256,256]{1,0:T(8,128)(2,1)}, u32[]{:S(2)}) copy-start(bf16[256,256]{1,0:T(8,128)(2,1)} %refs_0_.1) | copy-start | bytes 393220
  0.6 18.3 %collective-permute-start = (bf16[256,256]{1,0:T(8,128)(2,1)}, bf16[256,256]{1,0:T(8,128)(2,1)S(1)}, u32[]{:S(2)}, u32[]{:S(2)}) collective-permute-start(bf16[256,256]{1,0:T(8,128)(2,1)} %refs_0_.1), channel_id=1, source_target_pairs={{0,16},{2,18},{4,20},{6,22},{8,24},{10,26},{12,28},{14,30},{16,0},... | collective-permute-start | bytes 393224 | tf_op jit(solution)/shard_map/ppermute | solution.py:279
  18.9 30.2 %copy-start.5 = (bf16[256,256]{1,0:T(8,128)(2,1)}, bf16[256,256]{1,0:T(8,128)(2,1)S(1)}, u32[]{:S(2)}) copy-start(bf16[256,256]{1,0:T(8,128)(2,1)S(1)} %collective-permute-done.refs_1_) | copy-start | bytes 393220
  19.0 15.8 %copy-start.1 = (bf16[256,256]{1,0:T(8,128)(2,1)S(1)}, bf16[256,256]{1,0:T(8,128)(2,1)}, u32[]{:S(2)}) copy-start(bf16[256,256]{1,0:T(8,128)(2,1)} %refs_0_.1) | copy-start | bytes 393220
  19.0 15.8 %collective-permute-start.1 = (bf16[512,256]{1,0:T(8,128)(2,1)S(1)}, bf16[512,256]{1,0:T(8,128)(2,1)S(1)}, u32[]{:S(2)}, u32[]{:S(2)}) collective-permute-start(bf16[512,256]{1,0:T(8,128)(2,1)S(1)} %pad_maximum_fusion.3), channel_id=1, source_target_pairs={{0,8},{2,10},{4,12},{6,14},{8,0},{10,2},{12,4},{14,6},{16,24},{18,... | collective-permute-start | bytes 786440 | tf_op jit(solution)/shard_map/ppermute | solution.py:279
  34.8 19.5 %copy-start.3 = (bf16[512,256]{1,0:T(8,128)(2,1)}, bf16[512,256]{1,0:T(8,128)(2,1)S(1)}, u32[]{:S(2)}) copy-start(bf16[512,256]{1,0:T(8,128)(2,1)S(1)} %collective-permute-done.1.refs_2_) | copy-start | bytes 786436
  34.8 14.3 %collective-permute-start.3 = (bf16[1024,256]{1,0:T(8,128)(2,1)S(1)}, bf16[1024,256]{1,0:T(8,128)(2,1)S(1)}, u32[]{:S(2)}, u32[]{:S(2)}) collective-permute-start(bf16[1024,256]{1,0:T(8,128)(2,1)S(1)} %pad_maximum_fusion.1), channel_id=1, source_target_pairs={{0,4},{2,6},{4,0},{6,2},{8,12},{10,14},{12,8},{14,10},{16,20},{18,... | collective-permute-start | bytes 1572872 | tf_op jit(solution)/shard_map/ppermute | solution.py:279
  36.4 3.8 %collective-permute-start.2 = (f32[2,256]{1,0:T(2,128)}, f32[2,256]{1,0:T(2,128)S(1)}, u32[]{:S(2)}, u32[]{:S(2)}) collective-permute-start(f32[2,256]{1,0:T(2,128)} %row_stats.3), channel_id=1, source_target_pairs={{0,1},{1,0},{2,3},{3,2},{4,5},{5,4},{6,7},{7,6},{8,9},{9,8},{10,11... | collective-permute-start | bytes 6152 | tf_op jit(solution)/shard_map/ppermute | solution.py:279
  41.0 39.4 %copy-start.9 = (f32[1,256]{1,0:T(1,128)}, f32[1,256]{1,0:T(1,128)S(1)}, u32[]{:S(2)}) copy-start(f32[1,256]{1,0:T(1,128)S(1)} %add_add_fusion.lse_ref) | copy-start | bytes 3076
  41.0 4.5 %collective-permute-start.4 = (f32[1,1,256]{2,1,0:T(1,128)S(1)}, f32[1,1,256]{2,1,0:T(1,128)S(1)}, u32[]{:S(2)}, u32[]{:S(2)}) collective-permute-start(f32[1,1,256]{2,1,0:T(1,128)S(1)} %bitcast.7), channel_id=1, source_target_pairs={{0,16},{2,18},{4,20},{6,22},{8,24},{10,26},{12,28},{14,30},{16,0},... | collective-permute-start | bytes 3080 | tf_op jit(solution)/shard_map/ppermute | solution.py:279
  45.5 3.6 %collective-permute-start.5 = (f32[2,1,256]{2,1,0:T(1,128)S(1)}, f32[2,1,256]{2,1,0:T(1,128)S(1)}, u32[]{:S(2)}, u32[]{:S(2)}) collective-permute-start(f32[2,1,256]{2,1,0:T(1,128)S(1)} %pad_maximum_fusion.8), channel_id=1, source_target_pairs={{0,8},{2,10},{4,12},{6,14},{8,0},{10,2},{12,4},{14,6},{16,24},{18,... | collective-permute-start | bytes 6152 | tf_op jit(solution)/shard_map/ppermute | solution.py:279
  49.1 5.1 %copy-start.2 = (bf16[1024,256]{1,0:T(8,128)(2,1)}, bf16[1024,256]{1,0:T(8,128)(2,1)S(1)}, u32[]{:S(2)}) copy-start(bf16[1024,256]{1,0:T(8,128)(2,1)S(1)} %collective-permute-done.3.refs_3_) | copy-start | bytes 1572868
  49.2 5.0 %collective-permute-start.8 = (bf16[2048,256]{1,0:T(8,128)(2,1)S(1)}, bf16[2048,256]{1,0:T(8,128)(2,1)S(1)}, u32[]{:S(2)}, u32[]{:S(2)}) collective-permute-start(bf16[2048,256]{1,0:T(8,128)(2,1)S(1)} %pad_maximum_fusion), channel_id=1, source_target_pairs={{0,2},{2,0},{4,6},{6,4},{8,10},{10,8},{12,14},{14,12},{16,18},{18,... | collective-permute-start | bytes 3145736 | tf_op jit(solution)/shard_map/ppermute | solution.py:279
  49.3 3.7 %collective-permute-start.6 = (f32[4,1,256]{2,1,0:T(1,128)S(1)}, f32[4,1,256]{2,1,0:T(1,128)S(1)}, u32[]{:S(2)}, u32[]{:S(2)}) collective-permute-start(f32[4,1,256]{2,1,0:T(1,128)S(1)} %pad_maximum_fusion.7), channel_id=1, source_target_pairs={{0,4},{2,6},{4,0},{6,2},{8,12},{10,14},{12,8},{14,10},{16,20},{18,... | collective-permute-start | bytes 12296 | tf_op jit(solution)/shard_map/ppermute | solution.py:279
  53.0 1.2 collective-permute-start.7
  54.3 0.6 copy-start.8
  54.3 1.0 copy-start.4
  80.4 4.0 %collective-permute-start.9 = (f32[1,4096]{1,0:T(1,128)}, f32[1,4096]{1,0:T(1,128)S(1)}, u32[]{:S(2)}, u32[]{:S(2)}) collective-permute-start(f32[1,4096]{1,0:T(1,128)} %get-tuple-element.35), channel_id=1, source_target_pairs={{0,1},{1,0},{2,3},{3,2},{4,5},{5,4},{6,7},{7,6},{8,9},{9,8},{10,11... | collective-permute-start | bytes 49160 | tf_op jit(solution)/shard_map/ppermute | solution.py:279
  85.2 5.1 %collective-permute-start.10 = (f32[1,1,12288]{2,1,0:T(1,128)S(1)}, f32[1,1,12288]{2,1,0:T(1,128)S(1)}, u32[]{:S(2)}, u32[]{:S(2)}) collective-permute-start(f32[1,1,12288]{2,1,0:T(1,128)S(1)} %maximum_add_fusion), channel_id=1, source_target_pairs={{0,16},{2,18},{4,20},{6,22},{8,24},{10,26},{12,28},{14,30},{16,0},... | collective-permute-start | bytes 147464 | tf_op jit(solution)/shard_map/ppermute | solution.py:279
  90.3 4.7 %collective-permute-start.11 = (f32[2,1,12288]{2,1,0:T(1,128)S(1)}, f32[2,1,12288]{2,1,0:T(1,128)S(1)}, u32[]{:S(2)}, u32[]{:S(2)}) collective-permute-start(f32[2,1,12288]{2,1,0:T(1,128)S(1)} %pad_maximum_fusion.5), channel_id=1, source_target_pairs={{0,8},{2,10},{4,12},{6,14},{8,0},{10,2},{12,4},{14,6},{16,24},{18,... | collective-permute-start | bytes 294920 | tf_op jit(solution)/shard_map/ppermute | solution.py:279
  95.2 5.7 %collective-permute-start.12 = (f32[4,1,12288]{2,1,0:T(1,128)S(1)}, f32[4,1,12288]{2,1,0:T(1,128)S(1)}, u32[]{:S(2)}, u32[]{:S(2)}) collective-permute-start(f32[4,1,12288]{2,1,0:T(1,128)S(1)} %pad_maximum_fusion.4), channel_id=1, source_target_pairs={{0,4},{2,6},{4,0},{6,2},{8,12},{10,14},{12,8},{14,10},{16,20},{18,... | collective-permute-start | bytes 589832 | tf_op jit(solution)/shard_map/ppermute | solution.py:279
  101.3 1.8 %collective-permute-start.13 = (f32[8,1,12288]{2,1,0:T(1,128)S(1)}, f32[8,1,12288]{2,1,0:T(1,128)S(1)}, u32[]{:S(2)}, u32[]{:S(2)}) collective-permute-start(f32[8,1,12288]{2,1,0:T(1,128)S(1)} %pad_maximum_fusion.2), channel_id=1, source_target_pairs={{0,2},{2,0},{4,6},{6,4},{8,10},{10,8},{12,14},{14,12},{16,18},{18,... | collective-permute-start | bytes 1179656 | tf_op jit(solution)/shard_map/ppermute | solution.py:279
  103.2 0.9 copy-start.6
  127.4 29.3 %copy-start.7 = (f32[256,256]{1,0:T(8,128)S(1)}, f32[256,256]{1,0:T(8,128)}, u32[]{:S(2)}) copy-start(f32[256,256]{1,0:T(8,128)} %grad_rows.1) | copy-start | bytes 786436
  127.4 29.3 %collective-permute-start.14 = (f32[256,256]{1,0:T(8,128)}, f32[256,256]{1,0:T(8,128)S(1)}, u32[]{:S(2)}, u32[]{:S(2)}) collective-permute-start(f32[256,256]{1,0:T(8,128)} %grad_rows.1), channel_id=1, source_target_pairs={{0,1},{1,0},{2,3},{3,2},{4,5},{5,4},{6,7},{7,6},{8,9},{9,8},{10,11... | collective-permute-start | bytes 786440 | tf_op jit(solution)/shard_map/ppermute | solution.py:279
